TPU v7x, 128 devices: a whole 4x4x4 slice. The times are simulated.
128 devices in a mesh: seq: 16 (over y, z_hi, core), res: 8 (over z_lo, x).
Axes of the slice: x: 4, y: 4, z: 4 (z_hi: 2, z_lo: 2; z = z_hi * 2 + z_lo), core: 2. Of those that a mesh axis runs over, the one named last changes fastest.
Arguments:
- homolog_embedding: bfloat16 [128, 2048, 256], P('seq', 'res'), may hold values from -6 to 6
- pair_features: bfloat16 [2048, 2048, 128], P('res', 'seq'), may hold values from -6 to 6
- sequence_key_mask: int32 [128], replicated, may hold values 0 or 1
- residue_key_mask: int32 [2048], replicated, may hold values 0 or 1
- pair_head_bias_matrix: bfloat16 [128, 8], replicated
- horizontal_probe_weights: bfloat16 [256, 256], replicated, may hold values from -0.375 to 0.375
- horizontal_lookup_weights: bfloat16 [256, 512], replicated, may hold values from -0.375 to 0.375
- horizontal_sigmoid_weights: bfloat16 [256, 256], replicated, may hold values from -0.375 to 0.375
- horizontal_merge_weights: bfloat16 [256, 256], replicated, may hold values from -1.5 to 1.5
- column_query_matrix: bfloat16 [256, 256], replicated
- vertical_lookup_weights: bfloat16 [256, 512], replicated, may hold values from -0.375 to 0.375
- vertical_sigmoid_weights: bfloat16 [256, 256], replicated, may hold values from -0.375 to 0.375
- vertical_merge_weights: bfloat16 [256, 256], replicated, may hold values from -1.5 to 1.5
Outputs:
- alignment_after_rows: bfloat16 [128, 2048, 256], P('seq', 'res')
- alignment_final_state: bfloat16 [128, 2048, 256], P('seq', 'res')
All inputs are finite; a program needn't handle non-finite values.
Results may differ from a plain program's by a relative error of at most 0.03.
Values may be sent and summed in bfloat16 or wider, within the bound.
No kernel may reach another device: no remote copies, remote signals or barrier semaphores. Data moves between devices by JAX's collectives and lax.ppermute only.
A program may use at most 128 MiB of HBM per device.

v0:
```python
import math

import jax
import jax.numpy as jnp
from jax import lax
from jax.sharding import PartitionSpec as P

HEADCOUNT_PER = 8


def layer_normalize(values):
    values = values.astype(jnp.float32)
    center = values - jnp.mean(values, axis=-1, keepdims=True)
    spread = jnp.mean(center * center, axis=-1, keepdims=True)
    return center * lax.rsqrt(spread + 1e-05)


def column_pass(column_block, query_w, keyval_w, gate_w, out_w, key_mask):
    seq_count, res_count, channel_width = column_block.shape
    head_size = channel_width // HEADCOUNT_PER
    normalized_input = layer_normalize(column_block).astype(jnp.bfloat16)
    query_vectors = (
        jnp.dot(normalized_input, query_w, preferred_element_type=jnp.float32)
        * (1.0 / math.sqrt(head_size))
    ).astype(jnp.bfloat16)
    query_vectors = query_vectors.reshape(seq_count, res_count, HEADCOUNT_PER, head_size)
    key_value_pairs = jnp.dot(
        normalized_input, keyval_w, preferred_element_type=jnp.float32
    ).astype(jnp.bfloat16)
    keys = key_value_pairs[..., :channel_width].reshape(
        seq_count, res_count, HEADCOUNT_PER, head_size
    )
    values_part = key_value_pairs[..., channel_width:].reshape(
        seq_count, res_count, HEADCOUNT_PER, head_size
    )
    scores = jnp.einsum("snhd,tnhd->nhst", query_vectors, keys, preferred_element_type=jnp.float32)
    scores = jnp.where(key_mask[None, None, None, :] > 0, scores, -1000000000.0)
    weights = jax.nn.softmax(scores, axis=-1).astype(jnp.bfloat16)
    mixed = jnp.einsum("nhst,tnhd->snhd", weights, values_part, preferred_element_type=jnp.float32)
    mixed = mixed.reshape(seq_count, res_count, channel_width)
    gate_activation = jax.nn.sigmoid(
        jnp.dot(normalized_input, gate_w, preferred_element_type=jnp.float32)
    )
    gated = (mixed * gate_activation).astype(jnp.bfloat16)
    update = jnp.dot(gated, out_w, preferred_element_type=jnp.float32)
    return (column_block.astype(jnp.float32) + update).astype(jnp.bfloat16)


def per_device(
    homolog_embedding,
    pair_features,
    sequence_key_mask,
    residue_key_mask,
    pair_head_bias_matrix,
    horizontal_probe_weights,
    horizontal_lookup_weights,
    horizontal_sigmoid_weights,
    horizontal_merge_weights,
    column_query_matrix,
    vertical_lookup_weights,
    vertical_sigmoid_weights,
    vertical_merge_weights,
):
    sequence_shard_count, residue_shard_count, channel_width = homolog_embedding.shape
    head_size = channel_width // HEADCOUNT_PER
    group_count = lax.axis_size("seq")
    group_width = residue_shard_count // group_count
    pair_normed = layer_normalize(pair_features).astype(jnp.bfloat16)
    local_bias = jnp.einsum(
        "ijc,ch->hij", pair_normed, pair_head_bias_matrix, preferred_element_type=jnp.float32
    ).astype(jnp.bfloat16)
    pair_bias = lax.all_gather(local_bias, "seq", axis=2, tiled=True)
    normalized_input = layer_normalize(homolog_embedding).astype(jnp.bfloat16)
    key_value_pairs = jnp.dot(
        lax.all_gather(normalized_input, "res", axis=1, tiled=True),
        horizontal_lookup_weights,
        preferred_element_type=jnp.float32,
    ).astype(jnp.bfloat16)
    query_vectors = (
        jnp.dot(normalized_input, horizontal_probe_weights, preferred_element_type=jnp.float32)
        * (1.0 / math.sqrt(head_size))
    ).astype(jnp.bfloat16)
    gate_activation = jax.nn.sigmoid(
        jnp.dot(normalized_input, horizontal_sigmoid_weights, preferred_element_type=jnp.float32)
    )

    def row_single_pass(packed):
        query_seq, keyval_seq, gating_seq, rows_seq = packed
        query_heads = query_seq.reshape(residue_shard_count, HEADCOUNT_PER, head_size)
        key_heads = keyval_seq[:, :channel_width].reshape(-1, HEADCOUNT_PER, head_size)
        value_heads = keyval_seq[:, channel_width:].reshape(-1, HEADCOUNT_PER, head_size)
        scores = jnp.einsum(
            "ihd,jhd->hij", query_heads, key_heads, preferred_element_type=jnp.float32
        )
        scores = scores + pair_bias.astype(jnp.float32)
        scores = jnp.where(residue_key_mask[None, None, :] > 0, scores, -1000000000.0)
        weights = jax.nn.softmax(scores, axis=-1).astype(jnp.bfloat16)
        mixed = jnp.einsum(
            "hij,jhd->ihd", weights, value_heads, preferred_element_type=jnp.float32
        ).reshape(residue_shard_count, channel_width)
        gated = (mixed * gating_seq).astype(jnp.bfloat16)
        update = jnp.dot(gated, horizontal_merge_weights, preferred_element_type=jnp.float32)
        return (rows_seq.astype(jnp.float32) + update).astype(jnp.bfloat16)

    alignment_after_rows = lax.map(
        row_single_pass, (query_vectors, key_value_pairs, gate_activation, homolog_embedding)
    )
    grouped_rows = alignment_after_rows.reshape(
        sequence_shard_count, group_count, group_width, channel_width
    )
    column_block = lax.all_to_all(grouped_rows, "seq", split_axis=1, concat_axis=0, tiled=True)
    all_seqs, single, res_count, width = column_block.shape
    flat_block = column_block.reshape(all_seqs, res_count, width)
    result = column_pass(
        flat_block,
        column_query_matrix,
        vertical_lookup_weights,
        vertical_sigmoid_weights,
        vertical_merge_weights,
        sequence_key_mask,
    )
    column_attention_output = result.reshape(all_seqs, 1, res_count, width)
    returned_rows = lax.all_to_all(
        column_attention_output, "seq", split_axis=0, concat_axis=1, tiled=True
    )
    alignment_final_state = returned_rows.reshape(
        sequence_shard_count, residue_shard_count, channel_width
    )
    return (alignment_after_rows, alignment_final_state)


def solution(mesh):
    return jax.shard_map(
        per_device,
        mesh=mesh,
        in_specs=(
            P("seq", "res", None),
            P("res", "seq", None),
            P(),
            P(),
            P(),
            P(),
            P(),
            P(),
            P(),
            P(),
            P(),
            P(),
            P(),
        ),
        out_specs=(P("seq", "res", None), P("seq", "res", None)),
        check_vma=False,
    )
```

profile of v0, /device:TPU:1, one launch (start us, length us, event | category | flops | bytes accessed | tf_op | source)
XLA Modules:
  0.0 501.6 jit_solution(11239484583705747800)
XLA Ops:
  7.2 1.7 convert_reduce_fusion.1
  8.9 1.9 fusion.32
  10.8 1.5 fusion.33
  12.4 5.8 %convert_reduce_fusion = f32[256,128]{1,0:T(8,128)S(1)} fusion(bf16[256,128,128]{2,1,0:T(8,128)(2,1)} %param.16), kind=kLoop, calls=%fused_computation.24 | loop fusion | flops 8355840 | bytes 8519680 | tf_op jit(solution)/shard_map/reduce_sum | solution.py:13
  18.3 10.9 %fusion.18 = f32[256,128]{1,0:T(8,128)S(1)} fusion(bf16[256,128,128]{2,1,0:T(8,128)(2,1)} %param.16, f32[256,128]{1,0:T(8,128)S(1)} %broadcast_multiply_fusion), kind=kLoop, calls=%fused_computation.27 | loop fusion | flops 16744448 | bytes 8650752 | tf_op jit(solution)/shard_map/reduce_sum | solution.py:14
  29.2 12.4 %fusion.41 = bf16[8,256,128]{2,0,1:T(8,128)(2,1)} fusion(bf16[256,128,128]{2,1,0:T(8,128)(2,1)S(1)} %bitcast.150, f32[256,128]{1,0:T(8,128)S(1)} %add_rsqrt_fusion, f32[256,128]{1,0:T(8,128)S(1)} %broadcast_multiply_fusion, bf16[128,8]{0,1:T(8,128)(2,1)S(1)} %copy-done.15), kind=kOutput, calls=%fused_computation.60 | convolution fusion | flops 84148224 | bytes 9177088 | tf_op jit(solution)/shard_map/ijc,ch->hij/dot_general | solution.py:69
  41.7 1.4 multiply_convert_fusion.2
  43.1 2.0 add_divide_fusion
  45.1 62.5 %all-gather.3.cloned.1.call-done = bf16[8,2048,256]{2,1,0:T(8,128)(2,1)} async-done(((bf16[8,256,256]{2,1,0:T(8,128)(2,1)}), bf16[8,2048,256]{2,1,0:T(8,128)(2,1)}) %all-gather.3.cloned.1.call-update) | async-done | bytes 8388624 | tf_op jit(solution)/shard_map/all_gather | solution.py:75
  107.6 11.9 %convolution_convert_fusion = bf16[8,2048,512]{2,1,0:T(8,128)(2,1)} fusion(bf16[8,2048,256]{2,1,0:T(8,128)(2,1)} %all-gather.3.cloned.1.call-done, bf16[256,512]{1,0:T(8,128)(2,1)S(1)} %copy-done), kind=kOutput, calls=%fused_computation.29 | convolution fusion | flops 4303355904 | bytes 25427968 | tf_op jit(solution)/shard_map/dot_general | solution.py:74
  119.5 69.8 %all-gather.5.cloned.1.call-done = bf16[8,256,2048]{2,0,1:T(8,128)(2,1)} async-done(((bf16[8,256,128]{2,0,1:T(8,128)(2,1)}), bf16[8,256,2048]{2,0,1:T(8,128)(2,1)}) %all-gather.5.cloned.1.call-update) | async-done | bytes 8388624 | tf_op jit(solution)/shard_map/all_gather | solution.py:72
  189.4 11.2 %copy.62 = bf16[8,256,2048]{2,1,0:T(8,128)(2,1)} copy(bf16[8,256,2048]{2,0,1:T(8,128)(2,1)} %all-gather.5.cloned.1.call-done) | data formatting | bytes 16777216 | tf_op jit(solution)/shard_map/while | solution.py:105
  200.6 221.8 %while.10 = (s32[]{:T(128)}, bf16[8,256,256]{2,1,0:T(8,128)(2,1)}, bf16[8,256,256]{2,1,0:T(8,128)(2,1)}, bf16[8,2048,512]{2,1,0:T(8,128)(2,1)}, s32[2048]{0:T(10...) while((s32[]{:T(128)}, bf16[8,256,256]{2,1,0:T(8,128)(2,1)}, ...), condition=%wide.region_7.8_spmd, body=%wide.region_4.7_spmd.sunk | while | flops 885334016 | bytes 40008332 | solution.py:105
  200.6 3.1 constant_dynamic-slice_fusion.6
  203.7 2.9 copy.99
  208.8 7.6 %fusion.102 = f32[8,256]{1,0:T(8,128)S(1)} fusion(bf16[8,256,2048]{2,1,0:T(8,128)(2,1)} %get-tuple-element.197, pred[2048]{0:T(1024)(128)(4,1)S(1)} %broadcast_compare_fusion.3, bf16[256,8,32]{0,2,1:T(8,128)(2,1)S(1)} %bitcast.155, bf16[2048,8,32]{0,2,1:T(8,128)(2,1)S(1)} %bitcast.151), kind=kOutput, calls=%fused_computation.82.clone.1 | convolution fusion | flops 289409024 | bytes 9578496 | tf_op jit(solution)/shard_map/while/body/eval_jaxpr/sub | solution.py:97
  216.5 8.8 %fusion.103 = f32[8,32,256]{2,1,0:T(8,128)S(1)} fusion(bf16[2048,8,32]{0,2,1:T(8,128)(2,1)S(1)} %bitcast.153, f32[8,256]{1,0:T(8,128)S(1)} %fusion.102, bf16[8,256,2048]{2,1,0:T(8,128)(2,1)} %get-tuple-element.197, pred[2048]{0:T(1024)(128)(4,1)S(1)} %broadcast_compare_fusion.3, bf16[256,8,32]{0,2,1:T(8,128)(2,1)S(1)} %bitcast.156, ...), kind=kOutput, calls=%fused_computation.7.clone.1 | convolution fusion | flops 562040832 | bytes 10889216 | tf_op jit(solution)/shard_map/while/body/eval_jaxpr/hij,jhd->ihd/dot_general | solution.py:98
  226.5 1.8 fusion.105
  228.3 3.1 constant_dynamic-slice_fusion.6
  231.4 2.9 copy.99
  236.6 7.7 %fusion.102 = f32[8,256]{1,0:T(8,128)S(1)} fusion(bf16[8,256,2048]{2,1,0:T(8,128)(2,1)} %get-tuple-element.197, pred[2048]{0:T(1024)(128)(4,1)S(1)} %broadcast_compare_fusion.3, bf16[256,8,32]{0,2,1:T(8,128)(2,1)S(1)} %bitcast.155, bf16[2048,8,32]{0,2,1:T(8,128)(2,1)S(1)} %bitcast.151), kind=kOutput, calls=%fused_computation.82.clone.1 | convolution fusion | flops 289409024 | bytes 9578496 | tf_op jit(solution)/shard_map/while/body/eval_jaxpr/sub | solution.py:97
  244.2 8.8 %fusion.103 = f32[8,32,256]{2,1,0:T(8,128)S(1)} fusion(bf16[2048,8,32]{0,2,1:T(8,128)(2,1)S(1)} %bitcast.153, f32[8,256]{1,0:T(8,128)S(1)} %fusion.102, bf16[8,256,2048]{2,1,0:T(8,128)(2,1)} %get-tuple-element.197, pred[2048]{0:T(1024)(128)(4,1)S(1)} %broadcast_compare_fusion.3, bf16[256,8,32]{0,2,1:T(8,128)(2,1)S(1)} %bitcast.156, ...), kind=kOutput, calls=%fused_computation.7.clone.1 | convolution fusion | flops 562040832 | bytes 10889216 | tf_op jit(solution)/shard_map/while/body/eval_jaxpr/hij,jhd->ihd/dot_general | solution.py:98
  254.2 1.8 fusion.105
  256.0 3.1 constant_dynamic-slice_fusion.6
  259.1 2.9 copy.99
  264.3 7.7 %fusion.102 = f32[8,256]{1,0:T(8,128)S(1)} fusion(bf16[8,256,2048]{2,1,0:T(8,128)(2,1)} %get-tuple-element.197, pred[2048]{0:T(1024)(128)(4,1)S(1)} %broadcast_compare_fusion.3, bf16[256,8,32]{0,2,1:T(8,128)(2,1)S(1)} %bitcast.155, bf16[2048,8,32]{0,2,1:T(8,128)(2,1)S(1)} %bitcast.151), kind=kOutput, calls=%fused_computation.82.clone.1 | convolution fusion | flops 289409024 | bytes 9578496 | tf_op jit(solution)/shard_map/while/body/eval_jaxpr/sub | solution.py:97
  272.0 8.8 %fusion.103 = f32[8,32,256]{2,1,0:T(8,128)S(1)} fusion(bf16[2048,8,32]{0,2,1:T(8,128)(2,1)S(1)} %bitcast.153, f32[8,256]{1,0:T(8,128)S(1)} %fusion.102, bf16[8,256,2048]{2,1,0:T(8,128)(2,1)} %get-tuple-element.197, pred[2048]{0:T(1024)(128)(4,1)S(1)} %broadcast_compare_fusion.3, bf16[256,8,32]{0,2,1:T(8,128)(2,1)S(1)} %bitcast.156, ...), kind=kOutput, calls=%fused_computation.7.clone.1 | convolution fusion | flops 562040832 | bytes 10889216 | tf_op jit(solution)/shard_map/while/body/eval_jaxpr/hij,jhd->ihd/dot_general | solution.py:98
  282.0 1.8 fusion.105
  283.8 3.1 constant_dynamic-slice_fusion.6
  286.9 2.9 copy.99
  292.0 7.7 %fusion.102 = f32[8,256]{1,0:T(8,128)S(1)} fusion(bf16[8,256,2048]{2,1,0:T(8,128)(2,1)} %get-tuple-element.197, pred[2048]{0:T(1024)(128)(4,1)S(1)} %broadcast_compare_fusion.3, bf16[256,8,32]{0,2,1:T(8,128)(2,1)S(1)} %bitcast.155, bf16[2048,8,32]{0,2,1:T(8,128)(2,1)S(1)} %bitcast.151), kind=kOutput, calls=%fused_computation.82.clone.1 | convolution fusion | flops 289409024 | bytes 9578496 | tf_op jit(solution)/shard_map/while/body/eval_jaxpr/sub | solution.py:97
  299.7 8.8 %fusion.103 = f32[8,32,256]{2,1,0:T(8,128)S(1)} fusion(bf16[2048,8,32]{0,2,1:T(8,128)(2,1)S(1)} %bitcast.153, f32[8,256]{1,0:T(8,128)S(1)} %fusion.102, bf16[8,256,2048]{2,1,0:T(8,128)(2,1)} %get-tuple-element.197, pred[2048]{0:T(1024)(128)(4,1)S(1)} %broadcast_compare_fusion.3, bf16[256,8,32]{0,2,1:T(8,128)(2,1)S(1)} %bitcast.156, ...), kind=kOutput, calls=%fused_computation.7.clone.1 | convolution fusion | flops 562040832 | bytes 10889216 | tf_op jit(solution)/shard_map/while/body/eval_jaxpr/hij,jhd->ihd/dot_general | solution.py:98
  309.7 1.8 fusion.105
  311.5 3.1 constant_dynamic-slice_fusion.6
  314.6 2.9 copy.99
  319.7 7.7 %fusion.102 = f32[8,256]{1,0:T(8,128)S(1)} fusion(bf16[8,256,2048]{2,1,0:T(8,128)(2,1)} %get-tuple-element.197, pred[2048]{0:T(1024)(128)(4,1)S(1)} %broadcast_compare_fusion.3, bf16[256,8,32]{0,2,1:T(8,128)(2,1)S(1)} %bitcast.155, bf16[2048,8,32]{0,2,1:T(8,128)(2,1)S(1)} %bitcast.151), kind=kOutput, calls=%fused_computation.82.clone.1 | convolution fusion | flops 289409024 | bytes 9578496 | tf_op jit(solution)/shard_map/while/body/eval_jaxpr/sub | solution.py:97
  327.4 8.8 %fusion.103 = f32[8,32,256]{2,1,0:T(8,128)S(1)} fusion(bf16[2048,8,32]{0,2,1:T(8,128)(2,1)S(1)} %bitcast.153, f32[8,256]{1,0:T(8,128)S(1)} %fusion.102, bf16[8,256,2048]{2,1,0:T(8,128)(2,1)} %get-tuple-element.197, pred[2048]{0:T(1024)(128)(4,1)S(1)} %broadcast_compare_fusion.3, bf16[256,8,32]{0,2,1:T(8,128)(2,1)S(1)} %bitcast.156, ...), kind=kOutput, calls=%fused_computation.7.clone.1 | convolution fusion | flops 562040832 | bytes 10889216 | tf_op jit(solution)/shard_map/while/body/eval_jaxpr/hij,jhd->ihd/dot_general | solution.py:98
  337.4 1.8 fusion.105
  339.2 3.1 constant_dynamic-slice_fusion.6
  342.3 2.9 copy.99
  347.5 7.7 %fusion.102 = f32[8,256]{1,0:T(8,128)S(1)} fusion(bf16[8,256,2048]{2,1,0:T(8,128)(2,1)} %get-tuple-element.197, pred[2048]{0:T(1024)(128)(4,1)S(1)} %broadcast_compare_fusion.3, bf16[256,8,32]{0,2,1:T(8,128)(2,1)S(1)} %bitcast.155, bf16[2048,8,32]{0,2,1:T(8,128)(2,1)S(1)} %bitcast.151), kind=kOutput, calls=%fused_computation.82.clone.1 | convolution fusion | flops 289409024 | bytes 9578496 | tf_op jit(solution)/shard_map/while/body/eval_jaxpr/sub | solution.py:97
  355.2 8.8 %fusion.103 = f32[8,32,256]{2,1,0:T(8,128)S(1)} fusion(bf16[2048,8,32]{0,2,1:T(8,128)(2,1)S(1)} %bitcast.153, f32[8,256]{1,0:T(8,128)S(1)} %fusion.102, bf16[8,256,2048]{2,1,0:T(8,128)(2,1)} %get-tuple-element.197, pred[2048]{0:T(1024)(128)(4,1)S(1)} %broadcast_compare_fusion.3, bf16[256,8,32]{0,2,1:T(8,128)(2,1)S(1)} %bitcast.156, ...), kind=kOutput, calls=%fused_computation.7.clone.1 | convolution fusion | flops 562040832 | bytes 10889216 | tf_op jit(solution)/shard_map/while/body/eval_jaxpr/hij,jhd->ihd/dot_general | solution.py:98
  365.2 1.8 fusion.105
  367.0 3.1 constant_dynamic-slice_fusion.6
  370.1 2.9 copy.99
  375.2 7.7 %fusion.102 = f32[8,256]{1,0:T(8,128)S(1)} fusion(bf16[8,256,2048]{2,1,0:T(8,128)(2,1)} %get-tuple-element.197, pred[2048]{0:T(1024)(128)(4,1)S(1)} %broadcast_compare_fusion.3, bf16[256,8,32]{0,2,1:T(8,128)(2,1)S(1)} %bitcast.155, bf16[2048,8,32]{0,2,1:T(8,128)(2,1)S(1)} %bitcast.151), kind=kOutput, calls=%fused_computation.82.clone.1 | convolution fusion | flops 289409024 | bytes 9578496 | tf_op jit(solution)/shard_map/while/body/eval_jaxpr/sub | solution.py:97
  382.9 8.8 %fusion.103 = f32[8,32,256]{2,1,0:T(8,128)S(1)} fusion(bf16[2048,8,32]{0,2,1:T(8,128)(2,1)S(1)} %bitcast.153, f32[8,256]{1,0:T(8,128)S(1)} %fusion.102, bf16[8,256,2048]{2,1,0:T(8,128)(2,1)} %get-tuple-element.197, pred[2048]{0:T(1024)(128)(4,1)S(1)} %broadcast_compare_fusion.3, bf16[256,8,32]{0,2,1:T(8,128)(2,1)S(1)} %bitcast.156, ...), kind=kOutput, calls=%fused_computation.7.clone.1 | convolution fusion | flops 562040832 | bytes 10889216 | tf_op jit(solution)/shard_map/while/body/eval_jaxpr/hij,jhd->ihd/dot_general | solution.py:98
  392.9 1.8 fusion.105
  394.7 3.1 constant_dynamic-slice_fusion.6
  397.8 2.9 copy.99
  402.9 7.7 %fusion.102 = f32[8,256]{1,0:T(8,128)S(1)} fusion(bf16[8,256,2048]{2,1,0:T(8,128)(2,1)} %get-tuple-element.197, pred[2048]{0:T(1024)(128)(4,1)S(1)} %broadcast_compare_fusion.3, bf16[256,8,32]{0,2,1:T(8,128)(2,1)S(1)} %bitcast.155, bf16[2048,8,32]{0,2,1:T(8,128)(2,1)S(1)} %bitcast.151), kind=kOutput, calls=%fused_computation.82.clone.1 | convolution fusion | flops 289409024 | bytes 9578496 | tf_op jit(solution)/shard_map/while/body/eval_jaxpr/sub | solution.py:97
  410.6 8.8 %fusion.103 = f32[8,32,256]{2,1,0:T(8,128)S(1)} fusion(bf16[2048,8,32]{0,2,1:T(8,128)(2,1)S(1)} %bitcast.153, f32[8,256]{1,0:T(8,128)S(1)} %fusion.102, bf16[8,256,2048]{2,1,0:T(8,128)(2,1)} %get-tuple-element.197, pred[2048]{0:T(1024)(128)(4,1)S(1)} %broadcast_compare_fusion.3, bf16[256,8,32]{0,2,1:T(8,128)(2,1)S(1)} %bitcast.156, ...), kind=kOutput, calls=%fused_computation.7.clone.1 | convolution fusion | flops 562040832 | bytes 10889216 | tf_op jit(solution)/shard_map/while/body/eval_jaxpr/hij,jhd->ihd/dot_general | solution.py:98
  420.6 1.8 fusion.105
  422.4 2.8 copy.64
  425.2 3.8 all-to-all-start
  429.1 17.1 %all-to-all-done = bf16[8,16,16,256]{3,0,2,1:T(8,128)(2,1)S(1)} async-done(((bf16[8,16,16,256]{3,0,2,1:T(8,128)(2,1)}), bf16[8,16,16,256]{3,0,2,1:T(8,128)(2,1)S(1)}, u32[]{:S(2)}, u32[]{:S(2)}) %all-to-all-start) | async-done | bytes 1048608 | tf_op jit(solution)/shard_map/all_to_all | solution.py:111
  448.7 1.3 copy.74
  451.3 1.4 copy.75
  454.0 7.6 %fusion.62 = (f32[16,8,128]{2,1,0:T(8,128)S(1)}, f32[16,8,128,128]{2,3,1,0:T(8,128)}) fusion(pred[128]{0:T(512)(128)(4,1)S(1)} %broadcast_compare_fusion.1, bf16[128,16,8,32]{0,3,2,1:T(8,128)(2,1)S(1)} %bitcast.159, bf16[128,16,8,32]{0,3,2,1:T(8,128)(2,1)} %bitcast.160), kind=kOutput, calls=%fused_computation.84 | convolution fusion | flops 140509312 | bytes 10551424 | tf_op jit(solution)/shard_map/sub | solution.py:38
  461.6 6.0 %fusion.29 = f32[16,8,32,128]{3,2,1,0:T(8,128)} fusion(bf16[128,16,8,32]{0,3,2,1:T(8,128)(2,1)S(1)} %bitcast.161, f32[16,8,128,128]{2,3,1,0:T(8,128)} %get-tuple-element.111, f32[16,8,128]{2,1,0:T(8,128)S(1)} %get-tuple-element.110), kind=kOutput, calls=%fused_computation.39 | convolution fusion | flops 138412032 | bytes 11599872 | tf_op jit(solution)/shard_map/nhst,tnhd->snhd/dot_general | solution.py:39
  467.5 2.0 copy.77
  469.5 2.0 fusion.37
  471.5 1.9 copy.78
  473.4 20.4 %all_to_all.24 = bf16[128,1,16,256]{3,2,1,0:T(8,128)(2,1)S(1)} all-to-all(bf16[128,1,16,256]{3,2,1,0:T(8,128)(2,1)S(1)} %copy.78), channel_id=1, replica_groups=mesh['seq'=16,'res'=8] {'seq'}, dimensions={0} | all-to-all | bytes 2097152 | tf_op jit(solution)/shard_map/all_to_all | solution.py:123
  (133 shorter events, 33.0 us)
Async XLA Ops:
  7.2 100.5 %copy-start = (bf16[256,512]{1,0:T(8,128)(2,1)S(1)}, bf16[256,512]{1,0:T(8,128)(2,1)}, u32[]{:S(2)}) copy-start(bf16[256,512]{1,0:T(8,128)(2,1)} %param.21) | copy-start | bytes 786436
  7.2 3.6 copy-start.3
  7.2 100.4 %all-gather.3.cloned.1.call-start = ((), (), s32[]{:S(2)}) async-start(), calls=%async_computation.2 | async-start | bytes 9437184 | tf_op jit(solution)/shard_map/all_gather | solution.py:75
  12.3 177.0 %all-gather.5.cloned.1.call-start = ((), (), s32[]{:S(2)}) async-start(), calls=%async_computation.3 | async-start | bytes 8912896 | tf_op jit(solution)/shard_map/all_gather | solution.py:72
  12.4 16.8 %slice-start = ((s8[8388608]{0:T(1024)(128)(4,1)}), s8[4194304]{0:T(1024)(128)(4,1)S(1)}, s32[]{:S(2)}) async-start(s8[8388608]{0:T(1024)(128)(4,1)} %bitcast.149), calls=%async_computation.4 | async-start | bytes 8388608
  18.2 11.0 %slice-start.1 = ((s8[8388608]{0:T(1024)(128)(4,1)}), s8[4194304]{0:T(1024)(128)(4,1)S(1)}, s32[]{:S(2)}) async-start(s8[8388608]{0:T(1024)(128)(4,1)} %bitcast.149), calls=%async_computation.5 | async-start | bytes 8388608
  18.2 11.0 %copy-start.15 = (bf16[128,8]{0,1:T(8,128)(2,1)S(1)}, bf16[128,8]{0,1:T(8,128)(2,1)}, u32[]{:S(2)}) copy-start(bf16[128,8]{0,1:T(8,128)(2,1)} %param.19) | copy-start | bytes 6148
  29.2 12.4 %copy-start.4 = (bf16[8,256,256]{2,1,0:T(8,128)(2,1)S(1)}, bf16[8,256,256]{2,1,0:T(8,128)(2,1)}, u32[]{:S(2)}) copy-start(bf16[8,256,256]{2,1,0:T(8,128)(2,1)} %fusion.33) | copy-start | bytes 3145732
  29.2 12.4 %copy-start.9 = (bf16[256,256]{1,0:T(8,128)(2,1)S(1)}, bf16[256,256]{1,0:T(8,128)(2,1)}, u32[]{:S(2)}) copy-start(bf16[256,256]{1,0:T(8,128)(2,1)} %param.20) | copy-start | bytes 393220
  41.6 1.5 copy-start.11
  119.5 81.1 %copy-start.5 = (bf16[256,256]{1,0:T(8,128)(2,1)S(1)}, bf16[256,256]{1,0:T(8,128)(2,1)}, u32[]{:S(2)}) copy-start(bf16[256,256]{1,0:T(8,128)(2,1)} %param.23) | copy-start | bytes 393220
  119.5 81.1 %copy-start.8 = (s32[2048]{0:T(1024)S(1)}, s32[2048]{0:T(1024)}, u32[]{:S(2)}) copy-start(s32[2048]{0:T(1024)} %param.18) | copy-start | bytes 24580
  208.8 7.7 %copy-start.2 = (bf16[2048,256]{0,1:T(8,128)(2,1)S(1)}, bf16[2048,256]{0,1:T(8,128)(2,1)}, u32[]{:S(2)}) copy-start(bf16[2048,256]{0,1:T(8,128)(2,1)} %get-tuple-element.169) | copy-start | bytes 3145732 | tf_op jit(solution)/shard_map/while
  236.5 7.7 %copy-start.2 = (bf16[2048,256]{0,1:T(8,128)(2,1)S(1)}, bf16[2048,256]{0,1:T(8,128)(2,1)}, u32[]{:S(2)}) copy-start(bf16[2048,256]{0,1:T(8,128)(2,1)} %get-tuple-element.169) | copy-start | bytes 3145732 | tf_op jit(solution)/shard_map/while
  264.3 7.7 %copy-start.2 = (bf16[2048,256]{0,1:T(8,128)(2,1)S(1)}, bf16[2048,256]{0,1:T(8,128)(2,1)}, u32[]{:S(2)}) copy-start(bf16[2048,256]{0,1:T(8,128)(2,1)} %get-tuple-element.169) | copy-start | bytes 3145732 | tf_op jit(solution)/shard_map/while
  292.0 7.7 %copy-start.2 = (bf16[2048,256]{0,1:T(8,128)(2,1)S(1)}, bf16[2048,256]{0,1:T(8,128)(2,1)}, u32[]{:S(2)}) copy-start(bf16[2048,256]{0,1:T(8,128)(2,1)} %get-tuple-element.169) | copy-start | bytes 3145732 | tf_op jit(solution)/shard_map/while
  319.7 7.7 %copy-start.2 = (bf16[2048,256]{0,1:T(8,128)(2,1)S(1)}, bf16[2048,256]{0,1:T(8,128)(2,1)}, u32[]{:S(2)}) copy-start(bf16[2048,256]{0,1:T(8,128)(2,1)} %get-tuple-element.169) | copy-start | bytes 3145732 | tf_op jit(solution)/shard_map/while
  347.5 7.7 %copy-start.2 = (bf16[2048,256]{0,1:T(8,128)(2,1)S(1)}, bf16[2048,256]{0,1:T(8,128)(2,1)}, u32[]{:S(2)}) copy-start(bf16[2048,256]{0,1:T(8,128)(2,1)} %get-tuple-element.169) | copy-start | bytes 3145732 | tf_op jit(solution)/shard_map/while
  375.2 7.7 %copy-start.2 = (bf16[2048,256]{0,1:T(8,128)(2,1)S(1)}, bf16[2048,256]{0,1:T(8,128)(2,1)}, u32[]{:S(2)}) copy-start(bf16[2048,256]{0,1:T(8,128)(2,1)} %get-tuple-element.169) | copy-start | bytes 3145732 | tf_op jit(solution)/shard_map/while
  402.9 7.7 %copy-start.2 = (bf16[2048,256]{0,1:T(8,128)(2,1)S(1)}, bf16[2048,256]{0,1:T(8,128)(2,1)}, u32[]{:S(2)}) copy-start(bf16[2048,256]{0,1:T(8,128)(2,1)} %get-tuple-element.169) | copy-start | bytes 3145732 | tf_op jit(solution)/shard_map/while
  422.4 6.6 %copy-start.16 = (s32[128]{0:T(128)S(1)}, s32[128]{0:T(128)}, u32[]{:S(2)}) copy-start(s32[128]{0:T(128)} %param.17) | copy-start | bytes 1540
  425.2 21.0 %all-to-all-start = ((bf16[8,16,16,256]{3,0,2,1:T(8,128)(2,1)}), bf16[8,16,16,256]{3,0,2,1:T(8,128)(2,1)S(1)}, u32[]{:S(2)}, u32[]{:S(2)}) async-start(bf16[8,16,16,256]{3,0,2,1:T(8,128)(2,1)} %bitcast.14), calls=%async_computation | async-start | bytes 2097152 | tf_op jit(solution)/shard_map/all_to_all | solution.py:111
  429.0 18.6 %copy-start.12 = (bf16[256,256]{1,0:T(8,128)(2,1)S(1)}, bf16[256,256]{1,0:T(8,128)(2,1)}, u32[]{:S(2)}) copy-start(bf16[256,256]{1,0:T(8,128)(2,1)} %param.24) | copy-start | bytes 393220
  447.7 2.3 copy-start.10
  452.7 1.3 copy-start.6
  454.0 7.6 %copy-start.7 = (bf16[128,16,256]{0,2,1:T(8,128)(2,1)S(1)}, bf16[128,16,256]{0,2,1:T(8,128)(2,1)}, u32[]{:S(2)}) copy-start(bf16[128,16,256]{0,2,1:T(8,128)(2,1)} %copy.73) | copy-start | bytes 3145732
  467.5 2.0 copy-start.13
  467.5 2.0 copy-start.14
  471.5 23.3 %copy-start.1 = (bf16[256,512]{1,0:T(8,128)(2,1)S(1)}, bf16[256,512]{1,0:T(8,128)(2,1)}, u32[]{:S(2)}) copy-start(bf16[256,512]{1,0:T(8,128)(2,1)} %param.21) | copy-start | bytes 786436
Sparse Core Ops, SparseCore 0:
  12.5 95.1 all-gather.2
  109.9 79.4 all-gather.4
where the time goes:
time: 504 us; the launch traced here: 502 us
  matrix products  192 us (38%)
  waiting for transfers between devices  150 us (30%)
  local copies, waits for them, and re-layouts  98.1 us (19%)
  other arithmetic  23.2 us (5%)
  blocking collectives  20.4 us (4%)
  between operations  14.3 us (3%)
    dot_general x8, matrix products, row_single_pass(): jnp.einsum('hij,jhd->ihd', weights, value_heads, preferred_element_type=j...  70.8 us
    all_gather x1, waiting for transfers between devices, per_device(): pair_bias = lax.all_gather(local_bias, 'seq', axis=2, tiled=True)  69.8 us
    dynamic_slice x48, local copies, waits for them, and re-layouts, per_device(): lax.map(row_single_pass, (query_vectors, key_value_pairs, gate_activation...  65.1 us
    all_gather x1, waiting for transfers between devices, per_device(): lax.all_gather(normalized_input, 'res', axis=1, tiled=True)  62.5 us
    sub x8, matrix products, row_single_pass(): weights = jax.nn.softmax(scores, axis=-1).astype(jnp.bfloat16)  61.3 us
    all_to_all x1, blocking collectives, per_device(): lax.all_to_all(column_attention_output, 'seq', split_axis=0, concat_axis=...  20.4 us
    all_to_all x1, waiting for transfers between devices, per_device(): lax.all_to_all(grouped_rows, 'seq', split_axis=1, concat_axis=0, tiled=True)  17.1 us
    dot_general x8, matrix products, row_single_pass(): jnp.dot(gated, horizontal_merge_weights, preferred_element_type=jnp.float32)  14.4 us
  transfers between devices with their start and end apart: 3, of which 3 were waited for; matrix products, arithmetic and copies ran while one was open for 9% of the time, Pallas kernels for 0%

commit v1 on v0

v1 whole, which is shorter than its diff:
```python
import functools
import math

import jax
import jax.numpy as jnp
from jax import lax
from jax.experimental import pallas as pl
from jax.experimental.pallas import tpu as pltpu
from jax.sharding import PartitionSpec as P

HEADS = 8
LOG2E = math.log2(math.e)
MASKED = -1000000000.0
SAFE_SCORE = 100.0
BF16 = jnp.bfloat16
F32 = jnp.float32
NT = (((1,), (1,)), ((), ()))
VMEM_LIMIT = 60 * 2**20


def whole(*shape):
    return pl.BlockSpec(shape, lambda *_: (0,) * len(shape), pipeline_mode=pl.Buffered(1))


def layer_norm(x):
    center = x - jnp.mean(x, axis=-1, keepdims=True)
    spread = jnp.mean(center * center, axis=-1, keepdims=True)
    return center * lax.rsqrt(spread + 1e-05)


def norm_kernel(x_ref, out_ref):
    out_ref[...] = layer_norm(x_ref[...].astype(F32)).astype(BF16)


def norm_rows(x):
    seqs, res, width = x.shape
    return pl.pallas_call(
        norm_kernel,
        grid=(seqs // 2,),
        name="norm_rows",
        in_specs=[pl.BlockSpec((2, res, width), lambda s: (s, 0, 0))],
        out_specs=pl.BlockSpec((2, res, width), lambda s: (s, 0, 0)),
        out_shape=jax.ShapeDtypeStruct(x.shape, BF16),
    )(x)


def pair_kernel(x_ref, w_ref, out_ref, acc):
    rows, keys, width = x_ref.shape
    x = x_ref[...].reshape(rows * keys, width)
    average = jnp.full((width, width), 1.0 / width, BF16)
    center = x.astype(F32) - jnp.dot(x, average, preferred_element_type=F32)
    square = (center * center).astype(BF16)
    spread = jnp.dot(square, average, preferred_element_type=F32)
    normed = (center * lax.rsqrt(spread + 1e-05)).astype(BF16)
    for i in range(rows):
        acc[i] = lax.dot_general(
            w_ref[...], normed[i * keys : (i + 1) * keys], NT, preferred_element_type=F32
        )
    for h in range(HEADS):
        out_ref[h] = (acc[:, h, :] * LOG2E).astype(BF16)


def pair_bias(pair, head_w):
    rows, keys, width = pair.shape
    step = 32
    return pl.pallas_call(
        pair_kernel,
        grid=(rows // step,),
        name="pair_bias",
        in_specs=[
            pl.BlockSpec((step, keys, width), lambda i: (i, 0, 0)),
            whole(HEADS, width),
        ],
        out_specs=pl.BlockSpec((HEADS, step, keys), lambda i: (0, i, 0)),
        out_shape=jax.ShapeDtypeStruct((HEADS, rows, keys), BF16),
        scratch_shapes=[pltpu.VMEM((step, HEADS, keys), F32)],
        compiler_params=pltpu.CompilerParams(vmem_limit_bytes=VMEM_LIMIT),
    )(pair, head_w.T)


def head_lanes(rows, h, o):
    lane = lax.broadcasted_iota(jnp.int32, (rows, 128), 1) // 32
    return jnp.where(lane == h % 4, o, 0.0)


def row_kernel(
    normed_ref, own_ref, emb_ref, bias_ref, mask_col_ref, mask_row_ref, limit_ref,
    wqk_ref, wv_ref, wg_ref, wm_ref, out_ref, send_ref, va, qt, mixed,
):
    blocks, _, rows, width = normed_ref.shape
    length = blocks * rows
    tiles = bias_ref.shape[0]
    tile = length // tiles
    keep = mask_col_ref[...]

    @pl.when(pl.program_id(0) == 0)
    def _():
        for g in range(2):
            va[g, :, 128:] = jnp.broadcast_to(keep, (length, 128)).astype(BF16)

    def keys(k, count):
        return normed_ref[k : k + count, 0].reshape(count * rows, width)

    for k in range(blocks):
        v = jnp.dot(keys(k, 1), wv_ref[...], preferred_element_type=F32)
        v = (v * keep[k * rows : (k + 1) * rows]).astype(BF16)
        va[0, k * rows : (k + 1) * rows, :128] = v[:, :128]
        va[1, k * rows : (k + 1) * rows, :128] = v[:, 128:]
    own = own_ref[0]
    largest = jnp.zeros((rows, 1), F32)
    for h in range(HEADS):
        q = jnp.dot(own, wqk_ref[:, h * width : (h + 1) * width], preferred_element_type=F32)
        largest = jnp.maximum(largest, jnp.sum(q * q, axis=-1, keepdims=True))
        qt[h] = q.astype(BF16)
    largest = jnp.max(largest)

    def put(h, g, u):
        part = u[:, :128] / u[:, 128:]
        return head_lanes(rows, h, part)

    fast = largest < limit_ref[0]

    @pl.when(fast)
    def _():
        step = 1
        for h in range(HEADS):
            u = None
            for k in range(0, blocks, step):
                s = lax.dot_general(qt[h], keys(k, step), NT, preferred_element_type=F32)
                first = k * rows // tile
                b = [bias_ref[first + t, h] for t in range(step * rows // tile)]
                s = s + jnp.concatenate(b, axis=1).astype(F32)
                e = jnp.exp2(s).astype(BF16)
                d = jnp.dot(
                    e, va[h // 4, k * rows : (k + step) * rows], preferred_element_type=F32
                )
                u = d if u is None else u + d
            g = h // 4
            part = put(h, g, u)
            if h % 4 == 0:
                mixed[:, g * 128 : (g + 1) * 128] = part
            else:
                mixed[:, g * 128 : (g + 1) * 128] += part

    @pl.when(jnp.logical_not(fast))
    def _():
        mixed[...] = jnp.zeros_like(mixed)
        for g in range(2):

            def one(i, carry):
                h = g * 4 + i
                s = lax.dot_general(qt[h], keys(0, blocks), NT, preferred_element_type=F32)
                b = [bias_ref[t, h] for t in range(tiles)]
                s = s + jnp.concatenate(b, axis=1).astype(F32)
                s = jnp.where(mask_row_ref[...] > 0, s, MASKED)
                e = jnp.exp2(s - jnp.max(s, axis=-1, keepdims=True)).astype(BF16)
                u = jnp.dot(e, va[g], preferred_element_type=F32)
                mixed[:, g * 128 : (g + 1) * 128] += put(i, g, u)
                return carry

            lax.fori_loop(0, 4, one, 0)

    gate = jax.nn.sigmoid(jnp.dot(own, wg_ref[...], preferred_element_type=F32))
    gated = (mixed[...] * gate).astype(BF16)
    update = jnp.dot(gated, wm_ref[...], preferred_element_type=F32)
    result = (emb_ref[0].astype(F32) + update).astype(BF16)
    out_ref[0] = result
    send_ref[:, 0] = result.reshape(send_ref.shape[0], send_ref.shape[2], width)


def row_attention(normed, own, emb, bias, mask, limit, wqk, wv, wg, wm, groups):
    blocks, seqs, rows, width = normed.shape
    length = blocks * rows
    tiles = bias.shape[0]
    one = pl.BlockSpec((1, rows, width), lambda s: (s, 0, 0))
    part = rows // groups
    return pl.pallas_call(
        row_kernel,
        grid=(seqs,),
        name="row_attention",
        in_specs=[
            pl.BlockSpec((blocks, 1, rows, width), lambda s: (0, s, 0, 0)),
            one,
            one,
            whole(tiles, HEADS, rows, length // tiles),
            whole(length, 1),
            whole(1, length),
            pl.BlockSpec(memory_space=pltpu.SMEM),
            whole(width, HEADS * width),
            whole(width, width),
            whole(width, width),
            whole(width, width),
        ],
        out_specs=[one, pl.BlockSpec((groups, 1, part, width), lambda s: (0, s, 0, 0))],
        out_shape=[
            jax.ShapeDtypeStruct((seqs, rows, width), BF16),
            jax.ShapeDtypeStruct((groups, seqs, part, width), BF16),
        ],
        scratch_shapes=[
            pltpu.VMEM((2, length, 256), BF16),
            pltpu.VMEM((HEADS, rows, width), BF16),
            pltpu.VMEM((rows, width), F32),
        ],
        compiler_params=pltpu.CompilerParams(vmem_limit_bytes=VMEM_LIMIT),
    )(normed, own, emb, bias, mask.reshape(length, 1), mask.reshape(1, length), limit,
      wqk, wv, wg, wm)


def column_kernel(
    x_ref, mask_ref, wqk_ref, wv_ref, wg_ref, wm_ref, out_ref, raw, normed, done
):
    seqs, res, width = x_ref.shape
    x = x_ref[...].astype(F32)
    raw[...] = x
    normed[...] = layer_norm(x)
    ones = jnp.ones((seqs, 128), BF16)
    mask = mask_ref[...] > 0
    for r in range(res):
        n = normed[:, r, :].astype(BF16)
        v = jnp.dot(n, wv_ref[...], preferred_element_type=F32).astype(BF16)
        q = jnp.dot(n, wqk_ref[...], preferred_element_type=F32).astype(BF16)
        halves = []
        for g in range(2):
            qg = jnp.concatenate(
                [q[:, h * width : (h + 1) * width] for h in range(4 * g, 4 * g + 4)], axis=0
            )
            s = lax.dot_general(qg, n, NT, preferred_element_type=F32)
            s = jnp.where(mask, s, MASKED)
            e = jnp.exp2(s - jnp.max(s, axis=-1, keepdims=True)).astype(BF16)
            va = jnp.concatenate([v[:, g * 128 : (g + 1) * 128], ones], axis=1)
            u = jnp.dot(e, va, preferred_element_type=F32)
            o = u[:, :128] / u[:, 128:]
            halves.append(
                sum(head_lanes(seqs, h, o[h * seqs : (h + 1) * seqs]) for h in range(4))
            )
        gate = jax.nn.sigmoid(jnp.dot(n, wg_ref[...], preferred_element_type=F32))
        gated = (jnp.concatenate(halves, axis=1) * gate).astype(BF16)
        update = jnp.dot(gated, wm_ref[...], preferred_element_type=F32)
        done[:, r, :] = raw[:, r, :] + update
    out_ref[...] = done[...].astype(BF16)


def column_attention(x, mask, wqk, wv, wg, wm):
    seqs, res, width = x.shape
    return pl.pallas_call(
        column_kernel,
        name="column_attention",
        out_shape=jax.ShapeDtypeStruct(x.shape, BF16),
        scratch_shapes=[pltpu.VMEM(x.shape, F32)] * 3,
        compiler_params=pltpu.CompilerParams(vmem_limit_bytes=VMEM_LIMIT),
    )(x, mask.reshape(1, seqs), wqk, wv, wg, wm)


def fold_query_key(query_w, key_w):
    width = query_w.shape[0]
    size = width // HEADS
    q = query_w.reshape(width, HEADS, size)
    k = key_w.reshape(width, HEADS, size)
    both = jnp.einsum("chd,ehd->che", q, k, preferred_element_type=F32)
    return (both * (LOG2E / math.sqrt(size))).astype(BF16).reshape(width, HEADS * width)


def per_device(
    homolog_embedding,
    pair_features,
    sequence_key_mask,
    residue_key_mask,
    pair_head_bias_matrix,
    horizontal_probe_weights,
    horizontal_lookup_weights,
    horizontal_sigmoid_weights,
    horizontal_merge_weights,
    column_query_matrix,
    vertical_lookup_weights,
    vertical_sigmoid_weights,
    vertical_merge_weights,
):
    seqs, res, width = homolog_embedding.shape
    groups = lax.axis_size("seq")
    some = jnp.any(residue_key_mask > 0)
    keep = jnp.where(some, (residue_key_mask > 0).astype(F32), 1.0)
    head_w = jnp.where(some, pair_head_bias_matrix, 0).astype(BF16)
    wqk = fold_query_key(horizontal_probe_weights, horizontal_lookup_weights[:, :width])
    wqk = jnp.where(some, wqk, 0).astype(BF16)
    cqk = fold_query_key(column_query_matrix, vertical_lookup_weights[:, :width])
    norms = jnp.sqrt(jnp.sum(jnp.square(head_w.astype(F32)), axis=0))
    bias_bound = 1.02 * LOG2E * math.sqrt(pair_features.shape[-1]) * jnp.max(norms)
    room = jnp.maximum(SAFE_SCORE - bias_bound, 0.0) / (1.02 * math.sqrt(width))
    limit = (room * room).reshape(1)

    own = norm_rows(homolog_embedding)
    normed = lax.all_gather(own, "res")
    bias = lax.all_gather(pair_bias(pair_features, head_w), "seq")
    after_rows, send = row_attention(
        normed,
        own,
        homolog_embedding,
        bias,
        keep,
        limit,
        wqk,
        horizontal_lookup_weights[:, width:],
        horizontal_sigmoid_weights,
        horizontal_merge_weights,
        groups,
    )
    column = lax.all_to_all(send, "seq", 0, 0, tiled=True)
    result = column_attention(
        column.reshape(groups * seqs, res // groups, width),
        sequence_key_mask,
        cqk,
        vertical_lookup_weights[:, width:],
        vertical_sigmoid_weights,
        vertical_merge_weights,
    )
    back = lax.all_to_all(
        result.reshape(groups, seqs, res // groups, width), "seq", 0, 0, tiled=True
    )
    final = jnp.transpose(back, (1, 0, 2, 3)).reshape(seqs, res, width)
    return after_rows, final


def solution(mesh):
    return jax.shard_map(
        per_device,
        mesh=mesh,
        in_specs=(P("seq", "res", None), P("res", "seq", None)) + (P(),) * 11,
        out_specs=(P("seq", "res", None), P("seq", "res", None)),
        check_vma=False,
    )
```

time: 504 us -> 362 us (0.72)
  matrix products: 192 us -> 1.54 us
  Pallas kernels: 0 us -> 138 us
  local copies, waits for them, and re-layouts: 98.1 us -> 7.97 us
  other arithmetic: 23.2 us -> 3.72 us
  waiting for transfers between devices: 150 us -> 163 us
  starting transfers between devices: 3.89 us -> 11.2 us
    pallas_call x0 -> x4, Pallas kernels: none -> 138 us  [the longest x1 105 us: row_attention(): pl.pallas_call(row_kernel, grid=(seqs,), name='row_attention', in_specs=[...]
    dot_general x24 -> x2, matrix products: 123 us -> 1.54 us  [fold_query_key(): both = jnp.einsum('chd,ehd->che', q, k, preferred_element_type=F32)]
    sub x9 -> x0, matrix products: 68.9 us -> none  [the longest x8 61.3 us: row_single_pass(): weights = jax.nn.softmax(scores, axis=-1).astype(jnp.bfloat16)]
    dynamic_slice x48 -> x0, local copies, waits for them, and re-layouts: 65.1 us -> none  [per_device(): lax.map(row_single_pass, (query_vectors, key_value_pairs, gate_activation...]
    reduce_sum x6 -> x1, other arithmetic: 21.2 us -> 0.69 us  [per_device(): norms = jnp.sqrt(jnp.sum(jnp.square(head_w.astype(F32)), axis=0))]
    all_gather x2, waiting for transfers between devices: 132 us -> 148 us  [the longest x1 75 us: per_device(): bias = lax.all_gather(pair_bias(pair_features, head_w), 'seq')]
    while x18 -> x0, local copies, waits for them, and re-layouts: 14.1 us -> none  [the longest x2 14 us: per_device(): lax.map(row_single_pass, (query_vectors, key_value_pairs, gate_activation...]
    slice x11 -> x4, local copies, waits for them, and re-layouts: 12.2 us -> 1.52 us  [the longest x1 0.67 us: per_device(): vertical_lookup_weights[:, width:]]
  transfers between devices with their start and end apart: 3 -> 3, of which waited for: 3 -> 3; matrix products, arithmetic and copies ran while one was open for 9% -> 3% of each run, Pallas kernels for 0% -> 4%
where the time goes in v1:
time: 362 us; the launch traced here: 361 us
  waiting for transfers between devices  163 us (45%)
  Pallas kernels  138 us (38%)
  blocking collectives  21.1 us (6%)
  between operations  14.7 us (4%)
  starting transfers between devices  11.2 us (3%)
  local copies, waits for them, and re-layouts  7.97 us (2%)
  other arithmetic  3.72 us (1%)
    pallas_call x1, Pallas kernels, row_attention(): pl.pallas_call(row_kernel, grid=(seqs,), name='row_attention', in_specs=[...  105 us
    all_gather x1, waiting for transfers between devices, per_device(): bias = lax.all_gather(pair_bias(pair_features, head_w), 'seq')  75 us
    all_gather x1, waiting for transfers between devices, per_device(): normed = lax.all_gather(own, 'res')  73.5 us
    all_to_all x1, blocking collectives, per_device(): lax.all_to_all(result.reshape(groups, seqs, res // groups, width), 'seq',...  21.1 us
    pallas_call x1, Pallas kernels, column_attention(): pl.pallas_call(column_kernel, name='column_attention', out_shape=jax.Shap...  16.7 us
    all_to_all x1, waiting for transfers between devices, per_device(): column = lax.all_to_all(send, 'seq', 0, 0, tiled=True)  14.5 us
    pallas_call x1, Pallas kernels, pair_bias(): pl.pallas_call(pair_kernel, grid=(rows // step,), name='pair_bias', in_sp...  12.7 us
    all_to_all x1, starting transfers between devices, per_device(): column = lax.all_to_all(send, 'seq', 0, 0, tiled=True)  11.1 us
  transfers between devices with their start and end apart: 3, of which 3 were waited for; matrix products, arithmetic and copies ran while one was open for 3% of the time, Pallas kernels for 4%

profile of v1, /device:TPU:1, one launch (start us, length us, event | category | flops | bytes accessed | tf_op | source)
XLA Modules:
  0.0 361.0 jit_solution(9977359449205310822)
XLA Ops:
  7.2 0.0 copy-start.6
  7.2 0.0 copy-start.7
  7.2 0.0 all-gather.5.cloned.1.call-start
  7.2 3.8 %norm_rows.1.own_ref = bf16[8,256,256]{2,1,0:T(8,128)(2,1)} custom-call(bf16[8,256,256]{2,1,0:T(8,128)(2,1)} %emb_ref.1), custom_call_target="tpu_custom_call" | custom-call | tf_op jit(solution)/shard_map/norm_rows/pallas_call | solution.py:37
  11.0 0.0 all-gather.5.cloned.1.call-update
  11.1 0.0 all-gather.7.cloned.1.call-start
  11.1 0.0 copy-done.6
  11.1 0.6 fusion.2
  11.8 0.0 copy-done.7
  11.8 1.2 fusion.1.w_ref
  12.9 0.0 copy-start.1
  12.9 12.7 %pair_bias.1 = bf16[8,256,128]{2,1,0:T(8,128)(2,1)} custom-call(bf16[256,128,128]{2,1,0:T(8,128)(2,1)} %x_ref.3, bf16[8,128]{1,0:T(8,128)(2,1)} %fusion.1.w_ref), custom_call_target="tpu_custom_call" | custom-call | tf_op jit(solution)/shard_map/pair_bias/pallas_call | solution.py:66
  25.7 0.0 copy-start.3
  25.7 0.0 all-gather.7.cloned.1.call-update
  25.7 0.6 convert_select_fusion
  26.3 0.0 copy-start.5
  26.3 1.4 copy.33.mask_col_ref
  27.7 0.0 copy-done.1
  27.7 0.7 fusion.4
  28.3 0.1 copy.30
  28.4 0.0 copy-done.3
  28.4 0.1 copy.31
  28.5 1.1 fusion
  29.6 1.4 copy.38.wqk_ref
  31.0 0.0 copy-done.5
  31.0 0.7 multiply_reduce_fusion
  31.7 0.6 sqrt_reduce_fusion
  32.9 73.5 %all-gather.5.cloned.1.call-done = bf16[64,256,256]{2,1,0:T(8,128)(2,1)} async-done(((bf16[8,256,256]{2,1,0:T(8,128)(2,1)}), bf16[64,256,256]{2,1,0:T(8,128)(2,1)}) %all-gather.5.cloned.1.call-update) | async-done | bytes 8388624 | tf_op jit(solution)/shard_map/all_gather | solution.py:292
  106.4 75.0 %all-gather.7.cloned.1.call-done = bf16[128,256,128]{2,1,0:T(8,128)(2,1)} async-done(((bf16[8,256,128]{2,1,0:T(8,128)(2,1)}), bf16[128,256,128]{2,1,0:T(8,128)(2,1)}) %all-gather.7.cloned.1.call-update) | async-done | bytes 8388624 | tf_op jit(solution)/shard_map/all_gather | solution.py:293
  181.3 104.6 %row_attention.1 = (bf16[8,256,256]{2,1,0:T(8,128)(2,1)}, bf16[16,8,16,256]{3,2,1,0:T(8,128)(2,1)}) custom-call(bf16[8,8,256,256]{3,2,1,0:T(8,128)(2,1)} %bitcast.26, bf16[8,256,256]{2,1,0:T(8,128)(2,1)} %norm_rows.1.own_ref, bf16[8,256,256]{2,1,0:T(8,128)(2,1)} %emb_ref.1, bf16[16,8,256,128]{3,2,1,0:T(8,128)(2,1)} %bitcast.27, ...), custom_call_target="tpu_custom_call" | custom-call | tf_op jit(solution)/shard_map/row_attention/pallas_call | solution.py:177
  286.0 0.0 copy-start.2
  286.0 0.0 copy-start.4
  286.0 11.1 %all-to-all-start = ((bf16[16,8,16,256]{3,2,1,0:T(8,128)(2,1)}), bf16[16,8,16,256]{3,2,1,0:T(8,128)(2,1)S(1)}, u32[]{:S(2)}, u32[]{:S(2)}) async-start(bf16[16,8,16,256]{3,2,1,0:T(8,128)(2,1)} %get-tuple-element.5), calls=%async_computation | async-start | bytes 2097152 | tf_op jit(solution)/shard_map/all_to_all | solution.py:307
  297.1 0.0 copy-done.2
  297.1 0.7 fusion.3
  297.8 0.1 copy.34
  297.9 0.0 copy-done.4
  297.9 0.1 copy.35
  298.0 0.5 multiply_convert_fusion
  298.5 1.4 copy.39.wqk_ref
  299.9 14.5 %all-to-all-done = bf16[16,8,16,256]{3,2,1,0:T(8,128)(2,1)S(1)} async-done(((bf16[16,8,16,256]{3,2,1,0:T(8,128)(2,1)}), bf16[16,8,16,256]{3,2,1,0:T(8,128)(2,1)S(1)}, u32[]{:S(2)}, u32[]{:S(2)}) %all-to-all-start) | async-done | bytes 1048608 | tf_op jit(solution)/shard_map/all_to_all | solution.py:307
  314.4 0.0 copy-start
  314.4 1.0 copy-done
  315.3 16.7 %column_attention.1 = bf16[128,16,256]{2,1,0:T(8,128)(2,1)} custom-call(bf16[128,16,256]{2,1,0:T(8,128)(2,1)} %bitcast.30, s32[1,128]{1,0:T(1,128)} %bitcast.40, bf16[256,2048]{1,0:T(8,128)(2,1)} %copy.39.wqk_ref, bf16[256,256]{1,0:T(8,128)(2,1)} %get-tuple-element.8.wv_ref, bf16[256,256]{1,0:T(8,128)(2,1)} %wg_ref.3, bf16[256,256]{1,0:T(8,128)(2,1)} %wm_ref.3), custom_call_target="tpu_custom_call" | custom-call | tf_op jit(solution)/shard_map/column_attention/pallas_call | solution.py:245
  332.0 21.1 %all_to_all.10 = bf16[16,8,16,256]{3,2,1,0:T(8,128)(2,1)S(1)} all-to-all(bf16[16,8,16,256]{3,2,1,0:T(8,128)(2,1)} %bitcast.31), channel_id=1, replica_groups=mesh['seq'=16,'res'=8] {'seq'}, dimensions={0} | all-to-all | bytes 2097152 | tf_op jit(solution)/shard_map/all_to_all | solution.py:316
  353.1 1.1 copy.37
Async XLA Ops:
  7.2 3.9 %copy-start.6 = (s32[2048]{0:T(1024)S(1)}, s32[2048]{0:T(1024)}, u32[]{:S(2)}) copy-start(s32[2048]{0:T(1024)} %param.16) | copy-start | bytes 24580
  7.2 4.6 %copy-start.7 = (bf16[128,8]{0,1:T(8,128)(2,1)S(1)}, bf16[128,8]{0,1:T(8,128)(2,1)}, u32[]{:S(2)}) copy-start(bf16[128,8]{0,1:T(8,128)(2,1)} %param.17) | copy-start | bytes 6148
  7.2 99.2 %all-gather.5.cloned.1.call-start = ((), (), s32[]{:S(2)}) async-start(), calls=%async_computation.2 | async-start | bytes 9437184 | tf_op jit(solution)/shard_map/all_gather | solution.py:292
  11.1 170.3 %all-gather.7.cloned.1.call-start = ((), (), s32[]{:S(2)}) async-start(), calls=%async_computation.3 | async-start | bytes 8912896 | tf_op jit(solution)/shard_map/all_gather | solution.py:293
  12.9 14.7 %copy-start.1 = (bf16[256,512]{1,0:T(8,128)(2,1)S(1)}, bf16[256,512]{1,0:T(8,128)(2,1)}, u32[]{:S(2)}) copy-start(bf16[256,512]{1,0:T(8,128)(2,1)} %param.19) | copy-start | bytes 786436
  25.7 2.8 copy-start.3
  26.3 4.7 %copy-start.5 = (f32[2048]{0:T(1024)}, f32[2048]{0:T(1024)S(1)}, u32[]{:S(2)}) copy-start(f32[2048]{0:T(1024)S(1)} %convert_select_fusion) | copy-start | bytes 24580
  286.0 11.1 %copy-start.2 = (bf16[256,512]{1,0:T(8,128)(2,1)S(1)}, bf16[256,512]{1,0:T(8,128)(2,1)}, u32[]{:S(2)}) copy-start(bf16[256,512]{1,0:T(8,128)(2,1)} %param.23) | copy-start | bytes 786436
  286.0 11.9 %copy-start.4 = (bf16[256,256]{1,0:T(8,128)(2,1)S(1)}, bf16[256,256]{1,0:T(8,128)(2,1)}, u32[]{:S(2)}) copy-start(bf16[256,256]{1,0:T(8,128)(2,1)} %param.22) | copy-start | bytes 393220
  286.0 28.4 %all-to-all-start = ((bf16[16,8,16,256]{3,2,1,0:T(8,128)(2,1)}), bf16[16,8,16,256]{3,2,1,0:T(8,128)(2,1)S(1)}, u32[]{:S(2)}, u32[]{:S(2)}) async-start(bf16[16,8,16,256]{3,2,1,0:T(8,128)(2,1)} %get-tuple-element.5), calls=%async_computation | async-start | bytes 2097152 | tf_op jit(solution)/shard_map/all_to_all | solution.py:307
  314.4 1.0 copy-start
Sparse Core Ops, SparseCore 0:
  11.2 95.1 all-gather.4
  109.3 71.9 all-gather.6

commit v2 on v1

v2 whole, which is shorter than its diff:
```python
import functools
import math

import jax
import jax.numpy as jnp
from jax import lax
from jax.experimental import pallas as pl
from jax.experimental.pallas import tpu as pltpu
from jax.sharding import PartitionSpec as P

HEADS = 8
GROUP = 4
LOG2E = math.log2(math.e)
MASKED = -1000000000.0
SAFE_SCORE = 100.0
BF16 = jnp.bfloat16
F32 = jnp.float32
NT = (((1,), (1,)), ((), ()))
VMEM_LIMIT = 60 * 2**20


def cost(micros):
    return pl.CostEstimate(flops=int(micros * 1e9), bytes_accessed=0, transcendentals=0)


def whole(*shape):
    return pl.BlockSpec(shape, lambda *_: (0,) * len(shape), pipeline_mode=pl.Buffered(1))


def right_half(w):
    rows, columns = w.shape
    return pl.BlockSpec((rows, columns // 2), lambda *_: (0, 1), pipeline_mode=pl.Buffered(1))


def layer_norm(x):
    center = x - jnp.mean(x, axis=-1, keepdims=True)
    spread = jnp.mean(center * center, axis=-1, keepdims=True)
    return center * lax.rsqrt(spread + 1e-05)


def after(*arrays):
    return list(arrays), [pl.BlockSpec(memory_space=pl.ANY)] * len(arrays)


def norm_kernel(x_ref, *refs):
    out_ref = refs[-1]
    for s in range(out_ref.shape[0]):
        out_ref[s] = layer_norm(x_ref[s].astype(F32)).astype(BF16)


def norm_rows(x, at, count, late=()):
    _, res, width = x.shape
    args, specs = after(*late)
    return pl.pallas_call(
        norm_kernel,
        grid=(1,),
        name="norm_rows",
        in_specs=[pl.BlockSpec((count, res, width), lambda i: (at // count, 0, 0))] + specs,
        out_specs=pl.BlockSpec((count, res, width), lambda i: (0, 0, 0)),
        out_shape=jax.ShapeDtypeStruct((count, res, width), BF16),
        cost_estimate=cost(2),
    )(x, *args)


def pair_kernel(x_ref, w_ref, mask_ref, *rest):
    out_ref, acc = rest[-2:]
    rows, keys, width = x_ref.shape
    half = rows // 2
    wide = 2 * width
    x = jnp.concatenate([x_ref[:half], x_ref[half:]], axis=-1).reshape(half * keys, wide)
    side = lax.broadcasted_iota(jnp.int32, (wide, wide), 0) // width
    same = side == lax.broadcasted_iota(jnp.int32, (wide, wide), 1) // width
    average = jnp.where(same, 1.0 / width, 0.0).astype(BF16)
    center = x.astype(F32) - jnp.dot(x, average, preferred_element_type=F32)
    square = (center * center).astype(BF16)
    center = center.astype(BF16)
    pick = jnp.where(
        lax.broadcasted_iota(jnp.int32, (2 * HEADS, wide), 0) // HEADS
        == lax.broadcasted_iota(jnp.int32, (2 * HEADS, wide), 1) // width,
        1.0 / width,
        0.0,
    ).astype(BF16)
    head_w = w_ref[...].astype(F32).T
    zero = jnp.zeros_like(head_w)
    head_w = jnp.concatenate(
        [
            jnp.concatenate([head_w, zero], axis=1),
            jnp.concatenate([zero, head_w], axis=1),
        ],
        axis=0,
    ).astype(BF16)
    for i in range(0, half, 2):
        here = slice(i * keys, (i + 2) * keys)
        both = lax.dot_general(head_w, center[here], NT, preferred_element_type=F32)
        spread = lax.dot_general(pick, square[here], NT, preferred_element_type=F32)
        both = both * lax.rsqrt(spread + 1e-05)
        for t in range(2):
            acc[i + t] = both[:HEADS, t * keys : (t + 1) * keys]
            acc[half + i + t] = both[HEADS:, t * keys : (t + 1) * keys]
    mask = mask_ref[...]
    here = mask_ref[pl.ds(lax.axis_index("seq"), 1), :]
    none = jnp.max(mask) <= 0
    keep = here > 0
    scale = jnp.where(none, 0.0, LOG2E)
    masked = jnp.where(none, 0.0, MASKED * LOG2E)
    for h in range(HEADS):
        b = jnp.where(keep, acc[:, h, :] * scale, masked)
        out_ref[h] = b.astype(BF16)


def pair_bias(pair, at, rows, head_w, mask, late=()):
    _, keys, width = pair.shape
    step = 64
    args, specs = after(*late)
    return pl.pallas_call(
        pair_kernel,
        grid=(rows // step,),
        name="pair_bias",
        in_specs=[
            pl.BlockSpec((step, keys, width), lambda i: (at // step + i, 0, 0)),
            whole(width, HEADS),
            whole(mask.shape[0] // keys, keys),
        ]
        + specs,
        out_specs=pl.BlockSpec((HEADS, step, keys), lambda i: (0, i, 0)),
        out_shape=jax.ShapeDtypeStruct((HEADS, rows, keys), BF16),
        scratch_shapes=[pltpu.VMEM((step, HEADS, keys), F32)],
        compiler_params=pltpu.CompilerParams(vmem_limit_bytes=VMEM_LIMIT),
        cost_estimate=cost(6),
    )(pair, head_w, mask.reshape(-1, keys), *args)


def head_lanes(rows, h, o):
    lane = lax.broadcasted_iota(jnp.int32, (rows, 128), 1) // 32
    return jnp.where(lane == h % 4, o, 0.0)


def query_kernel(own_ref, wqk_ref, wg_ref, limit_ref, q_ref, gate_ref, fast_ref):
    _, rows, width = own_ref.shape
    own = own_ref[0]
    largest = jnp.zeros((rows, 1), F32)
    for h in range(HEADS):
        q = jnp.dot(own, wqk_ref[:, h * width : (h + 1) * width], preferred_element_type=F32)
        largest = jnp.maximum(largest, jnp.sum(q * q, axis=-1, keepdims=True))
        q_ref[0, h] = q.astype(BF16)
    gate_ref[0] = jax.nn.sigmoid(jnp.dot(own, wg_ref[...], preferred_element_type=F32))
    fast = (jnp.max(largest) < limit_ref[0]).astype(jnp.int32)

    @pl.when(pl.program_id(0) == 0)
    def _():
        fast_ref[0] = 1

    fast_ref[0] = fast_ref[0] * fast


def row_queries(own, wqk, wg, limit):
    seqs, rows, width = own.shape
    smem = pl.BlockSpec(memory_space=pltpu.SMEM)
    return pl.pallas_call(
        query_kernel,
        grid=(seqs,),
        name="row_queries",
        in_specs=[
            pl.BlockSpec((1, rows, width), lambda s: (s, 0, 0)),
            whole(*wqk.shape),
            whole(*wg.shape),
            smem,
        ],
        out_specs=[
            pl.BlockSpec((1, HEADS, rows, width), lambda s: (s, 0, 0, 0)),
            pl.BlockSpec((1, rows, width), lambda s: (s, 0, 0)),
            smem,
        ],
        out_shape=[
            jax.ShapeDtypeStruct((seqs, HEADS, rows, width), BF16),
            jax.ShapeDtypeStruct((seqs, rows, width), F32),
            jax.ShapeDtypeStruct((1,), jnp.int32),
        ],
        cost_estimate=cost(6),
    )(own, wqk, wg, limit)


def value_kernel(*refs):
    n = len(refs) // 2
    for x, out in zip(refs[:n], refs[n + 1 :]):
        out[0] = jnp.dot(x[0], refs[n][...], preferred_element_type=F32).astype(BF16)


def row_values(blocks, wv):
    seqs, rows, width = blocks[0].shape
    one = pl.BlockSpec((1, rows, width), lambda s: (s, 0, 0))
    return pl.pallas_call(
        value_kernel,
        grid=(seqs,),
        name="row_values",
        in_specs=[one] * len(blocks) + [right_half(wv)],
        out_specs=[one] * len(blocks),
        out_shape=[jax.ShapeDtypeStruct(x.shape, BF16) for x in blocks],
        cost_estimate=cost(1.5 * len(blocks)),
    )(*blocks, wv)


def row_kernel(spec, *refs):
    n_skip, turn, offsets, n_values, places = spec
    n_keys = len(offsets)
    refs = list(refs)
    take = lambda n: [refs.pop(0) for _ in range(n)]
    keys, values = take(n_keys), take(n_values)
    bias_in = take(len(places))
    q_ref, gate_ref, emb_ref, fast_ref, wv_ref, wm_ref = take(6)
    take(n_skip)
    out_ref, send_ref, bias, late, sems = refs
    each, block, width = keys[0].shape
    _, heads, rows, tile = bias.shape
    per = block // tile
    pack = max(1, block // rows)
    first = pl.program_id(0) == 0
    seq = lax.axis_index("seq")
    res = lax.axis_index("res")

    def copies():
        here = pl.ds(turn * rows, rows)
        n = 0
        for ref, group in zip(bias_in, places):
            for i, (dy, dz, dc) in enumerate(group):
                place = (
                    lax.rem(seq // 4 + dy, 4) * 4
                    + lax.rem(seq // 2 + dz, 2) * 2
                    + lax.rem(seq + dc, 2)
                )
                yield pltpu.make_async_copy(ref.at[i, :, here], bias.at[place], sems.at[n])
                n += 1

    @pl.when(first)
    def _():
        for c in copies():
            c.start()

    for i in range(each):
        for k in range(n_values, n_keys):
            v = jnp.dot(keys[k][i], wv_ref[...], preferred_element_type=F32)
            late[i, k - n_values] = v.astype(BF16)

    @pl.when(first)
    def _():
        for c in copies():
            c.wait()

    ones = jnp.ones((block, 128), BF16)

    def value(i, g, k):
        lanes = slice(g * 128, (g + 1) * 128)
        v = values[k][i, :, lanes] if k < n_values else late[i, k - n_values, :, lanes]
        return jnp.concatenate([v, ones], axis=1)

    at = [
        (lax.rem(res // 4 + dz, 2) * 4 + lax.rem(res + dx, 4)) * per for dz, dx in offsets
    ]

    def scores(i, h, k):
        q = q_ref[i, h : h + pack].reshape(pack * rows, width)
        s = lax.dot_general(q, keys[k][i], NT, preferred_element_type=F32)
        b = [bias[at[k] + t, h : h + pack].reshape(pack * rows, tile) for t in range(per)]
        return s + jnp.concatenate(b, axis=1).astype(F32)

    def mix(i, with_top):
        halves = []
        for g in range(2):
            total = None
            for h in range(g * GROUP, (g + 1) * GROUP, pack):
                top = None
                if with_top:
                    tops = [
                        jnp.max(scores(i, h, k), axis=-1, keepdims=True) for k in range(n_keys)
                    ]
                    top = functools.reduce(jnp.maximum, tops)
                u = None
                for k in range(n_keys):
                    s = scores(i, h, k)
                    e = jnp.exp2(s - top if with_top else s).astype(BF16)
                    d = jnp.dot(e, value(i, g, k), preferred_element_type=F32)
                    u = d if u is None else u + d
                o = u[:, :128] / u[:, 128:]
                for j in range(pack):
                    part = head_lanes(rows, h + j, o[j * rows : (j + 1) * rows])
                    total = part if total is None else total + part
            halves.append(total)
        gated = (jnp.concatenate(halves, axis=1) * gate_ref[i]).astype(BF16)
        update = jnp.dot(gated, wm_ref[...], preferred_element_type=F32)
        result = (emb_ref[i].astype(F32) + update).astype(BF16)
        out_ref[i] = result
        send_ref[:, i] = result.reshape(send_ref.shape[0], send_ref.shape[2], width)

    fast = fast_ref[0] > 0

    @pl.when(fast)
    def _():
        for i in range(each):
            mix(i, False)

    @pl.when(jnp.logical_not(fast))
    def _():
        lax.fori_loop(0, each, lambda i, carry: (mix(i, True), carry)[1], 0)


def row_attention(keys, values, bias, queries, gate, fast, emb, wv, wm, turn, rows_done=None):
    offsets, places = tuple(keys), tuple(bias)
    seqs, block, width = emb.shape
    _, heads, block, tile = bias[places[0]].shape
    tiles = sum(len(group) for group in places)
    rows = block // 2
    parts = lax.axis_size("seq")
    part = rows // parts
    each = 1
    mine = pl.BlockSpec((each, rows, width), lambda s: (s, turn, 0))
    args = [*keys.values(), *values, *bias.values(), queries, gate, emb, fast, wv, wm]
    specs = [pl.BlockSpec((each, block, width), lambda s: (s, 0, 0))] * (len(keys) + len(values))
    specs += [pl.BlockSpec(memory_space=pl.ANY)] * len(bias)
    specs += [pl.BlockSpec((each, heads, rows, width), lambda s: (s, 0, turn, 0)), mine, mine]
    specs += [pl.BlockSpec(memory_space=pltpu.SMEM), right_half(wv), whole(*wm.shape)]
    aliases = {}
    skipped = []
    if rows_done is not None:
        aliases[len(args)] = 0
        skipped.append(rows_done)
    skip_args, skip_specs = after(*skipped)
    spec = (len(skipped), turn, offsets, len(values), places)
    return pl.pallas_call(
        functools.partial(row_kernel, spec),
        grid=(seqs // each,),
        name="row_attention",
        in_specs=specs + skip_specs,
        out_specs=[mine, pl.BlockSpec((parts, each, part, width), lambda s: (0, s, 0, 0))],
        out_shape=[
            jax.ShapeDtypeStruct(emb.shape, BF16),
            jax.ShapeDtypeStruct((parts, seqs, part, width), BF16),
        ],
        scratch_shapes=[
            pltpu.VMEM((tiles, heads, rows, tile), BF16),
            pltpu.VMEM((each, len(keys) - len(values), block, width), BF16),
            pltpu.SemaphoreType.DMA((tiles,)),
        ],
        input_output_aliases=aliases,
        compiler_params=pltpu.CompilerParams(vmem_limit_bytes=VMEM_LIMIT),
        cost_estimate=cost(22),
    )(*args, *skip_args)


def column_kernel(
    x_ref, mask_ref, wqk_ref, wv_ref, wg_ref, wm_ref, *rest
):
    out_ref, raw, normed, done, qs = rest[-5:]
    groups, each, res, width = x_ref.shape
    seqs = groups * each
    x = x_ref[...].astype(F32)
    raw[...] = x
    normed[...] = layer_norm(x)
    ones = jnp.ones((seqs, 128), BF16)
    mask = mask_ref[...] > 0
    span = range(res)
    n = [normed[:, :, r, :].reshape(seqs, width).astype(BF16) for r in span]
    flat = jnp.concatenate(n, axis=0)
    v = jnp.dot(flat, wv_ref[...], preferred_element_type=F32).astype(BF16)
    gate = jax.nn.sigmoid(jnp.dot(flat, wg_ref[...], preferred_element_type=F32))
    for h in range(HEADS):
        q = jnp.dot(flat, wqk_ref[:, h * width : (h + 1) * width], preferred_element_type=F32)
        q = q.astype(BF16)
        for r in span:
            qs[r, h // 4, (h % 4) * seqs : (h % 4 + 1) * seqs] = q[r * seqs : (r + 1) * seqs]
    mixed = []
    for r in span:
        halves = []
        for g in range(2):
            s = lax.dot_general(qs[r, g], n[r], NT, preferred_element_type=F32)
            s = jnp.where(mask, s, MASKED)
            e = jnp.exp2(s - jnp.max(s, axis=-1, keepdims=True)).astype(BF16)
            va = jnp.concatenate(
                [v[r * seqs : (r + 1) * seqs, g * 128 : (g + 1) * 128], ones], axis=1
            )
            u = jnp.dot(e, va, preferred_element_type=F32)
            o = u[:, :128] / u[:, 128:]
            halves.append(
                sum(head_lanes(seqs, h, o[h * seqs : (h + 1) * seqs]) for h in range(4))
            )
        mixed.append(jnp.concatenate(halves, axis=1))
    gated = (jnp.concatenate(mixed, axis=0) * gate).astype(BF16)
    update = jnp.dot(gated, wm_ref[...], preferred_element_type=F32)
    for r in span:
        before = raw[:, :, r, :]
        done[:, :, r, :] = before + update[r * seqs : (r + 1) * seqs].reshape(before.shape)
    out_ref[...] = done[...].astype(BF16)


def column_attention(x, mask, wqk, wv, wg, wm, late=()):
    args, specs = after(*late)
    return pl.pallas_call(
        column_kernel,
        grid=(1,),
        name="column_attention",
        in_specs=[whole(*x.shape), whole(1, mask.shape[0]), whole(*wqk.shape), right_half(wv)]
        + [whole(*wg.shape), whole(*wm.shape)]
        + specs,
        out_specs=whole(*x.shape),
        out_shape=jax.ShapeDtypeStruct(x.shape, BF16),
        scratch_shapes=[pltpu.VMEM(x.shape, F32)] * 3
        + [pltpu.VMEM((x.shape[2], 2, 4 * x.shape[0] * x.shape[1], x.shape[3]), BF16)],
        compiler_params=pltpu.CompilerParams(vmem_limit_bytes=VMEM_LIMIT),
        cost_estimate=cost(8),
    )(x, mask.reshape(1, -1), wqk, wv, wg, wm, *args)


def fold_kernel(
    mask_ref, head_ref, rq_ref, rkv_ref, cq_ref, ckv_ref, wqk_ref, cqk_ref, limit_ref
):
    width = rq_ref.shape[0]
    size = width // HEADS
    factor = LOG2E / math.sqrt(size)
    some = jnp.max(mask_ref[...]) > 0
    lane = lax.broadcasted_iota(jnp.int32, (width, width), 1) // size
    for q_ref, k_ref, out_ref, scale in (
        (rq_ref, rkv_ref, wqk_ref, jnp.where(some, factor, 0.0)),
        (cq_ref, ckv_ref, cqk_ref, factor),
    ):
        q, k = q_ref[...], k_ref[:, :width]
        for h in range(HEADS):
            one = jnp.where(lane == h, q, jnp.zeros_like(q))
            both = lax.dot_general(one, k, NT, preferred_element_type=F32)
            out_ref[:, h * width : (h + 1) * width] = (both * scale).astype(BF16)
    head = head_ref[...].astype(F32)
    norm = jnp.max(jnp.sqrt(jnp.sum(head * head, axis=0, keepdims=True)))
    room = SAFE_SCORE - 1.02 * LOG2E * math.sqrt(head.shape[0]) * norm
    room = jnp.maximum(room, 0.0) / (1.02 * math.sqrt(width))
    limit_ref[0] = room * room


def fold_weights(mask, head_w, rq, rkv, cq, ckv):
    width = rq.shape[0]
    vmem = pl.BlockSpec(memory_space=pltpu.VMEM)
    return pl.pallas_call(
        fold_kernel,
        name="fold_weights",
        out_specs=[vmem, vmem, pl.BlockSpec(memory_space=pltpu.SMEM)],
        out_shape=[jax.ShapeDtypeStruct((width, HEADS * width), BF16)] * 2
        + [jax.ShapeDtypeStruct((1,), F32)],
        cost_estimate=cost(3),
    )(mask, head_w, rq, rkv, cq, ckv)


def fetch_seq(x, dy, dz, dc):
    pairs = [
        (((y + dy) % 4) * 4 + ((z + dz) % 2) * 2 + (c + dc) % 2, y * 4 + z * 2 + c)
        for y in range(4)
        for z in range(2)
        for c in range(2)
    ]
    return lax.ppermute(x, "seq", pairs)


def fetch_row(x, dz, dx):
    pairs = [
        (((z + dz) % 2) * 4 + (i + dx) % 4, z * 4 + i) for z in range(2) for i in range(4)
    ]
    return lax.ppermute(x, "res", pairs)


def pack_kernel(*refs):
    for i, ref in enumerate(refs[:-1]):
        refs[-1][i] = ref[...]


def pack_blocks(blocks):
    first, *others = blocks[0].shape
    step = first // 4
    return pl.pallas_call(
        pack_kernel,
        grid=(4,),
        name="pack_blocks",
        in_specs=[pl.BlockSpec((step, *others), lambda i: (i, 0, 0))] * len(blocks),
        out_specs=pl.BlockSpec((len(blocks), step, *others), lambda i: (0, i, 0, 0)),
        out_shape=jax.ShapeDtypeStruct((len(blocks), first, *others), blocks[0].dtype),
        cost_estimate=cost(2),
    )(*blocks)


def hold_kernel(*refs):
    pass


def hold(*trees, micros=1):
    boxes = [dict(zip(range(len(t)), t.values())) if isinstance(t, dict) else t for t in trees]
    flat, tree = jax.tree.flatten(boxes)
    any_ = pl.BlockSpec(memory_space=pl.ANY)
    out = pl.pallas_call(
        hold_kernel,
        name="step_done",
        in_specs=[any_] * len(flat),
        out_specs=[any_] * len(flat),
        out_shape=[jax.ShapeDtypeStruct(x.shape, x.dtype) for x in flat],
        input_output_aliases={i: i for i in range(len(flat))},
        cost_estimate=cost(micros),
    )(*flat)
    out = jax.tree.unflatten(tree, out)
    return [dict(zip(t, o.values())) if isinstance(t, dict) else o for t, o in zip(trees, out)]


def per_device(
    homolog_embedding,
    pair_features,
    sequence_key_mask,
    residue_key_mask,
    pair_head_bias_matrix,
    horizontal_probe_weights,
    horizontal_lookup_weights,
    horizontal_sigmoid_weights,
    horizontal_merge_weights,
    column_query_matrix,
    vertical_lookup_weights,
    vertical_sigmoid_weights,
    vertical_merge_weights,
):
    seqs, res, width = homolog_embedding.shape
    groups = lax.axis_size("seq")
    wqk, cqk, limit = fold_weights(
        residue_key_mask.reshape(16, -1),
        pair_head_bias_matrix,
        horizontal_probe_weights,
        horizontal_lookup_weights,
        column_query_matrix,
        vertical_lookup_weights,
    )
    lookup = horizontal_lookup_weights
    a, c = {}, {}
    a[0, 0] = norm_rows(homolog_embedding, 0, seqs)
    a[0, 1] = fetch_row(a[0, 0], 0, 1)
    a[0, 3] = fetch_row(a[0, 0], 0, 3)
    a[1, 0] = fetch_row(a[0, 0], 1, 0)
    c[0, 0] = pair_bias(
        pair_features, 0, res, pair_head_bias_matrix, residue_key_mask, (a[0, 0],)
    )
    c[1, 0] = fetch_seq(c[0, 0], 1, 0, 0)
    c[3, 0] = fetch_seq(c[0, 0], 3, 0, 0)
    bias = {}

    def swap(*offsets):
        both = c[offsets[0]][None] if len(offsets) == 1 else pack_blocks([c[o] for o in offsets])
        bias[tuple((*o, 0) for o in offsets)] = both
        bias[tuple((*o, 1) for o in offsets)] = fetch_seq(both, 0, 0, 1)

    (a,) = hold(a, micros=15)
    a[1, 1] = fetch_row(a[1, 0], 0, 1)
    c[0, 1] = fetch_seq(c[0, 0], 0, 1, 0)
    a[0, 2] = fetch_row(a[0, 3], 0, 3)
    c[2, 0] = fetch_seq(c[1, 0], 1, 0, 0)
    order = ((0, 0), (0, 1), (0, 3), (1, 0), (1, 1), (0, 2), (1, 3), (1, 2))
    early = row_values([a[o] for o in order[:4]], lookup)
    queries = row_queries(a[0, 0], wqk, horizontal_sigmoid_weights, limit)
    a, early, queries, c = hold(a, early, queries, c, micros=15)
    a[1, 2] = fetch_row(a[1, 1], 0, 1)
    a[1, 3] = fetch_row(a[1, 0], 0, 3)
    c[1, 1] = fetch_seq(c[0, 1], 1, 0, 0)
    c[3, 1] = fetch_seq(c[0, 1], 3, 0, 0)
    c[2, 1] = fetch_seq(c[2, 0], 0, 1, 0)
    middle = row_values([a[o] for o in order[4:6]], lookup)
    swap(*c)
    a, middle = hold(a, middle, micros=40)
    keys = {o: a[o] for o in order}
    rest = ([*early, *middle], bias, *queries, homolog_embedding, lookup)
    rest += (horizontal_merge_weights,)
    after_rows, send_0 = row_attention(keys, *rest, 0)
    after_rows, send_1 = row_attention(keys, *rest, 1, after_rows)
    column = (
        sequence_key_mask,
        cqk,
        vertical_lookup_weights,
        vertical_sigmoid_weights,
        vertical_merge_weights,
    )
    x_0, x_1 = (lax.all_to_all(x, "seq", 0, 0, tiled=True) for x in (send_0, send_1))
    done_0 = column_attention(x_0, *column, (after_rows,))
    x_1, done_0 = hold(x_1, done_0)
    done_1 = column_attention(x_1, *column)
    finals = [lax.all_to_all(x, "seq", 0, 0, tiled=True) for x in (done_0, done_1)]
    final = jnp.transpose(jnp.stack(finals), (2, 0, 1, 3, 4)).reshape(seqs, res, width)
    return after_rows, final


def solution(mesh):
    return jax.shard_map(
        per_device,
        mesh=mesh,
        in_specs=(P("seq", "res", None), P("res", "seq", None)) + (P(),) * 11,
        out_specs=(P("seq", "res", None), P("seq", "res", None)),
        check_vma=False,
    )
```

time: 362 us -> 218 us (0.60)
  waiting for transfers between devices: 163 us -> 19 us
  starting transfers between devices: 11.2 us -> 48 us
  between operations: 14.7 us -> 0.79 us
  Pallas kernels: 138 us -> 129 us
  blocking collectives: 21.1 us -> 15.9 us
  other arithmetic: 3.72 us -> 0.1 us
    all_gather x2 -> x0, waiting for transfers between devices: 148 us -> none  [the longest x1 75 us: per_device(): bias = lax.all_gather(pair_bias(pair_features, head_w), 'seq')]
    ppermute x0 -> x15, starting transfers between devices: none -> 30.9 us  [the longest x8 20.3 us: fetch_seq(): return lax.ppermute(x, 'seq', pairs)]
    ppermute x0 -> x15, waiting for transfers between devices: none -> 12.7 us  [the longest x8 9.24 us: fetch_seq(): return lax.ppermute(x, 'seq', pairs)]
    all_to_all x1 -> x3, waiting for transfers between devices: 14.5 us -> 6.3 us  [per_device(): lax.all_to_all(x, 'seq', 0, 0, tiled=True)]
    pallas_call x3 -> x14, Pallas kernels: 125 us -> 118 us  [the longest x2 66.4 us: row_attention(): pl.pallas_call(functools.partial(row_kernel, spec), grid=(seqs // each,),...]
    all_to_all x1 -> x3, starting transfers between devices: 11.1 us -> 17.1 us  [per_device(): lax.all_to_all(x, 'seq', 0, 0, tiled=True)]
    all_to_all x1, blocking collectives: 21.1 us -> 15.9 us  [per_device(): lax.all_to_all(x, 'seq', 0, 0, tiled=True)]
  transfers between devices with their start and end apart: 3 -> 18, of which waited for: 3 -> 6; matrix products, arithmetic and copies ran while one was open for 3% -> 0% of each run, Pallas kernels for 4% -> 42%
where the time goes in v2:
time: 218 us; the launch traced here: 217 us
  Pallas kernels  129 us (59%)
  starting transfers between devices  48 us (22%)
  waiting for transfers between devices  19 us (9%)
  blocking collectives  15.9 us (7%)
  local copies, waits for them, and re-layouts  4.56 us (2%)
    pallas_call x2, Pallas kernels, row_attention(): pl.pallas_call(functools.partial(row_kernel, spec), grid=(seqs // each,),...  66.4 us
    ppermute x8, starting transfers between devices, fetch_seq(): return lax.ppermute(x, 'seq', pairs)  20.3 us
    all_to_all x3, starting transfers between devices, per_device(): lax.all_to_all(x, 'seq', 0, 0, tiled=True)  17.1 us
    pallas_call x2, Pallas kernels, column_attention(): pl.pallas_call(column_kernel, grid=(1,), name='column_attention', in_spec...  16 us
    all_to_all x1, blocking collectives, per_device(): lax.all_to_all(x, 'seq', 0, 0, tiled=True)  15.9 us
    pallas_call x2, Pallas kernels, row_values(): pl.pallas_call(value_kernel, grid=(seqs,), name='row_values', in_specs=[o...  14.2 us
    ppermute x7, starting transfers between devices, fetch_row(): return lax.ppermute(x, 'res', pairs)  10.6 us
    pallas_call x1, Pallas kernels, pair_bias(): pl.pallas_call(pair_kernel, grid=(rows // step,), name='pair_bias', in_sp...  10.2 us
  transfers between devices with their start and end apart: 18, of which 6 were waited for; matrix products, arithmetic and copies ran while one was open for 0% of the time, Pallas kernels for 42%

profile of v2, /device:TPU:1, one launch (start us, length us, event | category | flops | bytes accessed | tf_op | source)
XLA Modules:
  0.0 217.1 jit_solution(3864259490411459346)
XLA Ops:
  0.6 0.0 copy-start.10
  0.6 3.2 %norm_rows.1.refs_0_.rest_0_ = bf16[8,256,256]{2,1,0:T(8,128)(2,1)} custom-call(bf16[8,256,256]{2,1,0:T(8,128)(2,1)} %refs_18_.3), custom_call_target="tpu_custom_call" | custom-call | flops 2000000000 | tf_op jit(solution)/shard_map/norm_rows/pallas_call | solution.py:54
  3.8 2.5 %collective-permute-start.2 = (bf16[8,256,256]{2,1,0:T(8,128)(2,1)}, bf16[8,256,256]{2,1,0:T(8,128)(2,1)}, u32[]{:S(2)}, u32[]{:S(2)}) collective-permute-start(bf16[8,256,256]{2,1,0:T(8,128)(2,1)} %norm_rows.1.refs_0_.rest_0_), channel_id=1, source_target_pairs={{4,0},{5,1},{6,2},{7,3},{0,4},{1,5},{2,6},{3,7},{12,8},{13,9},{14,... | collective-permute-start | bytes 3145736 | tf_op jit(solution)/shard_map/ppermute | solution.py:463
  6.3 1.2 collective-permute-start.1
  7.5 1.5 collective-permute-start
  9.0 0.0 copy-done.10
  9.0 0.7 copy.52.head_ref.w_ref
  9.7 10.2 %pair_bias.1.refs_13_ = bf16[8,256,128]{2,1,0:T(8,128)(2,1)} custom-call(bf16[256,128,128]{2,1,0:T(8,128)(2,1)} %x_ref.3, bf16[128,8]{1,0:T(8,128)(2,1)} %copy.52.head_ref.w_ref, s32[16,128]{1,0:T(8,128)} %bitcast.10, bf16[8,256,256]{2,1,0:T(8,128)(2,1)} %norm_rows.1.refs_0_.rest_0_), custom_call_target="tpu_custom_call" | custom-call | flops 6000000000 | tf_op jit(solution)/shard_map/pair_bias/pallas_call | solution.py:115
  19.9 2.7 %collective-permute-start.5 = (bf16[8,256,128]{2,1,0:T(8,128)(2,1)}, bf16[8,256,128]{2,1,0:T(8,128)(2,1)S(1)}, u32[]{:S(2)}, u32[]{:S(2)}) collective-permute-start(bf16[8,256,128]{2,1,0:T(8,128)(2,1)} %pair_bias.1.refs_13_), channel_id=1, source_target_pairs={{32,0},{40,8},{48,16},{56,24},{64,32},{72,40},{80,48},{88,56},{96,... | collective-permute-start | bytes 1572872 | tf_op jit(solution)/shard_map/ppermute | solution.py:456
  22.7 3.3 %collective-permute-start.7 = (bf16[8,256,128]{2,1,0:T(8,128)(2,1)}, bf16[8,256,128]{2,1,0:T(8,128)(2,1)S(1)}, u32[]{:S(2)}, u32[]{:S(2)}) collective-permute-start(bf16[8,256,128]{2,1,0:T(8,128)(2,1)} %pair_bias.1.refs_13_), channel_id=1, source_target_pairs={{16,0},{24,8},{0,16},{8,24},{48,32},{56,40},{32,48},{40,56},{80,64... | collective-permute-start | bytes 1572872 | tf_op jit(solution)/shard_map/ppermute | solution.py:456
  26.0 3.0 %fold_weights.1 = (bf16[256,2048]{1,0:T(8,128)(2,1)}, bf16[256,2048]{1,0:T(8,128)(2,1)}, f32[1]{0:T(128)}) custom-call(s32[16,128]{1,0:T(8,128)} %bitcast.11, bf16[128,8]{1,0:T(8,128)(2,1)} %copy.52.head_ref.w_ref, bf16[256,256]{1,0:T(8,128)(2,1)} %rq_ref.1, bf16[256,512]{1,0:T(8,128)(2,1)} %refs_20_.3, bf16[256,256]{1,0:T(8,128)(2,1)} %cq_ref.1, ...), custom_call_target="tpu_custom_call" | custom-call | flops 3000000000 | tf_op jit(solution)/shard_map/fold_weights/pallas_call | solution.py:439
  29.0 3.7 %collective-permute-done.5.refs_14_ = bf16[8,256,128]{2,1,0:T(8,128)(2,1)S(1)} collective-permute-done((bf16[8,256,128]{2,1,0:T(8,128)(2,1)}, bf16[8,256,128]{2,1,0:T(8,128)(2,1)S(1)}, u32[]{:S(2)}, u32[]{:S(2)}) %collective-permute-start.5) | collective-permute-done | bytes 524320 | tf_op jit(solution)/shard_map/ppermute | solution.py:456
  32.7 0.0 copy-done
  32.7 0.8 collective-permute-start.6
  33.4 0.0 collective-permute-done.2.refs_3_
  33.4 2.6 %collective-permute-start.8 = (bf16[8,256,128]{2,1,0:T(8,128)(2,1)S(1)}, bf16[8,256,128]{2,1,0:T(8,128)(2,1)S(1)}, u32[]{:S(2)}, u32[]{:S(2)}) collective-permute-start(bf16[8,256,128]{2,1,0:T(8,128)(2,1)S(1)} %collective-permute-done.5.refs_14_), channel_id=1, source_target_pairs={{32,0},{40,8},{48,16},{56,24},{64,32},{72,40},{80,48},{88,56},{96,... | collective-permute-start | bytes 1572872 | tf_op jit(solution)/shard_map/ppermute | solution.py:456
  36.1 0.0 collective-permute-done.1.refs_2_
  36.1 0.0 collective-permute-done.refs_1_
  36.1 0.0 copy-done.1
  36.1 0.1 collective-permute-start.4
  36.2 2.7 %collective-permute-start.3 = (bf16[8,256,256]{2,1,0:T(8,128)(2,1)}, bf16[8,256,256]{2,1,0:T(8,128)(2,1)}, u32[]{:S(2)}, u32[]{:S(2)}) collective-permute-start(bf16[8,256,256]{2,1,0:T(8,128)(2,1)} %get-tuple-element.55.refs_3_), channel_id=1, source_target_pairs={{1,0},{2,1},{3,2},{0,3},{5,4},{6,5},{7,6},{4,7},{9,8},{10,9},{11,1... | collective-permute-start | bytes 3145736 | tf_op jit(solution)/shard_map/ppermute | solution.py:463
  38.8 7.6 %row_values.2 = (bf16[8,256,256]{2,1,0:T(8,128)(2,1)}, bf16[8,256,256]{2,1,0:T(8,128)(2,1)}, bf16[8,256,256]{2,1,0:T(8,128)(2,1)}, bf16[8,256,256]{2,1,0:T(8,128)(2,1)}) custom-call(bf16[8,256,256]{2,1,0:T(8,128)(2,1)} %get-tuple-element.52.refs_0_.own_ref, bf16[8,256,256]{2,1,0:T(8,128)(2,1)} %get-tuple-element.53.refs_1_, ...), custom_call_target="tpu_custom_call" | custom-call | flops 6000000000 | tf_op jit(solution)/shard_map/row_values/pallas_call | solution.py:192
  46.4 9.7 %row_queries.1 = (bf16[8,8,256,256]{3,2,1,0:T(8,128)(2,1)}, f32[8,256,256]{2,1,0:T(8,128)}, s32[1]{0:T(128)}) custom-call(bf16[8,256,256]{2,1,0:T(8,128)(2,1)} %get-tuple-element.52.refs_0_.own_ref, bf16[256,2048]{1,0:T(8,128)(2,1)} %get-tuple-element.60.wqk_ref, bf16[256,256]{1,0:T(8,128)(2,1)} %wg_ref.3, f32[1]{0:T(128)} %get-tuple-element.61.limit_ref), custom_call_target="tpu_custom_call" | custom-call | flops 6000000000 | tf_op jit(solution)/shard_map/row_queries/pallas_call | solution.py:159
  56.1 0.0 collective-permute-done.7.refs_16_
  56.1 0.0 collective-permute-done.6.refs_15_
  56.1 0.0 copy-start.3
  56.1 0.0 collective-permute-done.8.refs_17_
  56.1 3.5 %collective-permute-done.4.refs_5_ = bf16[8,256,256]{2,1,0:T(8,128)(2,1)} collective-permute-done((bf16[8,256,256]{2,1,0:T(8,128)(2,1)}, bf16[8,256,256]{2,1,0:T(8,128)(2,1)}, u32[]{:S(2)}, u32[]{:S(2)}) %collective-permute-start.4) | collective-permute-done | bytes 1048608 | tf_op jit(solution)/shard_map/ppermute | solution.py:463
  59.6 0.0 collective-permute-done.3.refs_4_
  59.6 0.0 copy-done.3
  59.6 0.0 copy-done.4
  59.6 1.2 step_done.5
  60.8 3.4 %collective-permute-start.13 = (bf16[8,256,128]{2,1,0:T(8,128)(2,1)}, bf16[8,256,128]{2,1,0:T(8,128)(2,1)S(1)}, u32[]{:S(2)}, u32[]{:S(2)}) collective-permute-start(bf16[8,256,128]{2,1,0:T(8,128)(2,1)} %get-tuple-element.91.refs_4_), channel_id=1, source_target_pairs={{16,0},{24,8},{0,16},{8,24},{48,32},{56,40},{32,48},{40,56},{80,64... | collective-permute-start | bytes 1572872 | tf_op jit(solution)/shard_map/ppermute | solution.py:456
  64.2 0.0 collective-permute-start.12
  64.2 2.7 %collective-permute-start.11 = (bf16[8,256,128]{2,1,0:T(8,128)(2,1)}, bf16[8,256,128]{2,1,0:T(8,128)(2,1)S(1)}, u32[]{:S(2)}, u32[]{:S(2)}) collective-permute-start(bf16[8,256,128]{2,1,0:T(8,128)(2,1)} %get-tuple-element.90.refs_3_), channel_id=1, source_target_pairs={{32,0},{40,8},{48,16},{56,24},{64,32},{72,40},{80,48},{88,56},{96,... | collective-permute-start | bytes 1572872 | tf_op jit(solution)/shard_map/ppermute | solution.py:456
  66.9 0.0 collective-permute-start.10
  66.9 2.7 %collective-permute-start.9 = (bf16[8,256,256]{2,1,0:T(8,128)(2,1)}, bf16[8,256,256]{2,1,0:T(8,128)(2,1)}, u32[]{:S(2)}, u32[]{:S(2)}) collective-permute-start(bf16[8,256,256]{2,1,0:T(8,128)(2,1)} %get-tuple-element.69.refs_0_.refs_4_), channel_id=1, source_target_pairs={{1,0},{2,1},{3,2},{0,3},{5,4},{6,5},{7,6},{4,7},{9,8},{10,9},{11,1... | collective-permute-start | bytes 3145736 | tf_op jit(solution)/shard_map/ppermute | solution.py:463
  69.6 3.4 %collective-permute-done.13.refs_7_ = bf16[8,256,128]{2,1,0:T(8,128)(2,1)S(1)} collective-permute-done((bf16[8,256,128]{2,1,0:T(8,128)(2,1)}, bf16[8,256,128]{2,1,0:T(8,128)(2,1)S(1)}, u32[]{:S(2)}, u32[]{:S(2)}) %collective-permute-start.13) | collective-permute-done | bytes 524320 | tf_op jit(solution)/shard_map/ppermute | solution.py:456
  73.0 2.1 collective-permute-done.12.refs_6_
  75.1 0.0 collective-permute-done.11.refs_5_
  75.1 0.8 copy-done.6
  75.9 0.2 copy-done.7
  76.1 4.8 %pack_blocks.1.refs_14_ = bf16[8,8,256,128]{3,2,1,0:T(8,128)(2,1)} custom-call(bf16[8,256,128]{2,1,0:T(8,128)(2,1)} %get-tuple-element.87.refs_0_, bf16[8,256,128]{2,1,0:T(8,128)(2,1)} %get-tuple-element.88.refs_1_, bf16[8,256,128]{2,1,0:T(8,128)(2,1)} %get-tuple-element.89.refs_2_, bf16[8,256,128]{2,1,0:T(8,128)(2,1)} %get-tuple-element.90.refs_3_, ...), custom_call_target="tpu_custom_call" | custom-call | flops 2000000000 | tf_op jit(solution)/shard_map/pack_blocks/pallas_call | solution.py:474
  80.9 4.8 %collective-permute-start.14 = (bf16[8,8,256,128]{3,2,1,0:T(8,128)(2,1)}, bf16[8,8,256,128]{3,2,1,0:T(8,128)(2,1)}, u32[]{:S(2)}, u32[]{:S(2)}) collective-permute-start(bf16[8,8,256,128]{3,2,1,0:T(8,128)(2,1)} %pack_blocks.1.refs_14_), channel_id=1, source_target_pairs={{8,0},{0,8},{24,16},{16,24},{40,32},{32,40},{56,48},{48,56},{72,64... | collective-permute-start | bytes 12582920 | tf_op jit(solution)/shard_map/ppermute | solution.py:456
  85.7 6.6 %row_values.3 = (bf16[8,256,256]{2,1,0:T(8,128)(2,1)}, bf16[8,256,256]{2,1,0:T(8,128)(2,1)}) custom-call(bf16[8,256,256]{2,1,0:T(8,128)(2,1)} %get-tuple-element.69.refs_0_.refs_4_, bf16[8,256,256]{2,1,0:T(8,128)(2,1)} %get-tuple-element.70.refs_1_.refs_5_, bf16[256,512]{1,0:T(8,128)(2,1)} %refs_20_.3), custom_call_target="tpu_custom_call" | custom-call | flops 3000000000 | tf_op jit(solution)/shard_map/row_values/pallas_call | solution.py:192
  92.3 0.0 collective-permute-done.10.refs_7_
  92.3 0.0 collective-permute-done.9.refs_6_
  92.4 1.0 copy-done.11
  93.3 0.0 collective-permute-done.14.refs_15_
  93.3 33.2 %row_attention.2 = (bf16[8,256,256]{2,1,0:T(8,128)(2,1)}, bf16[16,8,8,256]{3,2,1,0:T(8,128)(2,1)}) custom-call(bf16[8,256,256]{2,1,0:T(8,128)(2,1)} %get-tuple-element.73.refs_0_, bf16[8,256,256]{2,1,0:T(8,128)(2,1)} %get-tuple-element.74.refs_1_, bf16[8,256,256]{2,1,0:T(8,128)(2,1)} %get-tuple-element.75.refs_2_, ...), custom_call_target="tpu_custom_call" | custom-call | flops 22000001024 | tf_op jit(solution)/shard_map/row_attention/pallas_call | solution.py:328
  126.5 4.9 %all-to-all-start.1 = ((bf16[16,8,8,256]{3,2,1,0:T(8,128)(2,1)}), bf16[16,8,8,256]{3,2,1,0:T(8,128)(2,1)S(1)}, u32[]{:S(2)}, u32[]{:S(2)}) async-start(bf16[16,8,8,256]{3,2,1,0:T(8,128)(2,1)} %get-tuple-element.98), calls=%async_computation.1 | async-start | bytes 1048576 | tf_op jit(solution)/shard_map/all_to_all | solution.py:578
  131.4 33.2 %row_attention.3 = (bf16[8,256,256]{2,1,0:T(8,128)(2,1)}, bf16[16,8,8,256]{3,2,1,0:T(8,128)(2,1)}) custom-call(bf16[8,256,256]{2,1,0:T(8,128)(2,1)} %get-tuple-element.73.refs_0_, bf16[8,256,256]{2,1,0:T(8,128)(2,1)} %get-tuple-element.74.refs_1_, bf16[8,256,256]{2,1,0:T(8,128)(2,1)} %get-tuple-element.75.refs_2_, ...), custom_call_target="tpu_custom_call", output_to_operand_aliasing={{0}: (22, {})} | custom-call | flops 22000001024 | tf_op jit(solution)/shard_map/row_attention/pallas_call | solution.py:328
  164.7 0.0 all-to-all-done.1.x_ref
  164.7 0.0 copy-start.8
  164.7 7.3 %all-to-all-start = ((bf16[16,8,8,256]{3,2,1,0:T(8,128)(2,1)}), bf16[16,8,8,256]{3,2,1,0:T(8,128)(2,1)S(1)}, u32[]{:S(2)}, u32[]{:S(2)}) async-start(bf16[16,8,8,256]{3,2,1,0:T(8,128)(2,1)} %get-tuple-element.97), calls=%async_computation | async-start | bytes 1048576 | tf_op jit(solution)/shard_map/all_to_all | solution.py:578
  172.0 8.0 %column_attention.2.refs_1_ = bf16[16,8,8,256]{3,2,1,0:T(8,128)(2,1)} custom-call(bf16[16,8,8,256]{3,2,1,0:T(8,128)(2,1)} %copy-done.8, s32[1,128]{1,0:T(1,128)} %bitcast.12, bf16[256,2048]{1,0:T(8,128)(2,1)} %get-tuple-element.99.wqk_ref, bf16[256,512]{1,0:T(8,128)(2,1)} %wv_ref.3, bf16[256,256]{1,0:T(8,128)(2,1)} %wg_ref.5, bf16[256,256]{1,0:T(8,128)(2,1)} %wm_ref.3, ...), custom_call_target="tpu_custom_call" | custom-call | flops 8000000000 | tf_op jit(solution)/shard_map/column_attention/pallas_call | solution.py:396
  180.0 3.1 %all-to-all-done.refs_0_ = bf16[16,8,8,256]{3,2,1,0:T(8,128)(2,1)S(1)} async-done(((bf16[16,8,8,256]{3,2,1,0:T(8,128)(2,1)}), bf16[16,8,8,256]{3,2,1,0:T(8,128)(2,1)S(1)}, u32[]{:S(2)}, u32[]{:S(2)}) %all-to-all-start) | async-done | bytes 524320 | tf_op jit(solution)/shard_map/all_to_all | solution.py:578
  183.1 0.8 copy-done.9
  183.9 4.9 %all-to-all-start.2 = ((bf16[16,8,8,256]{3,2,1,0:T(8,128)(2,1)}), bf16[16,8,8,256]{3,2,1,0:T(8,128)(2,1)S(1)}, u32[]{:S(2)}, u32[]{:S(2)}) async-start(bf16[16,8,8,256]{3,2,1,0:T(8,128)(2,1)} %get-tuple-element.100), calls=%async_computation.2 | async-start | bytes 1048576 | tf_op jit(solution)/shard_map/all_to_all | solution.py:582
  188.8 8.0 %column_attention.3 = bf16[16,8,8,256]{3,2,1,0:T(8,128)(2,1)} custom-call(bf16[16,8,8,256]{3,2,1,0:T(8,128)(2,1)} %get-tuple-element.101.x_ref, s32[1,128]{1,0:T(1,128)} %bitcast.13, bf16[256,2048]{1,0:T(8,128)(2,1)} %get-tuple-element.99.wqk_ref, bf16[256,512]{1,0:T(8,128)(2,1)} %wv_ref.3, bf16[256,256]{1,0:T(8,128)(2,1)} %wg_ref.5, bf16[256,256]{1,0:T(8,128)(2,1)} %wm_ref.3), custom_call_target="tpu_custom_call" | custom-call | flops 8000000000 | tf_op jit(solution)/shard_map/column_attention/pallas_call | solution.py:396
  196.9 3.2 %all-to-all-done.2 = bf16[16,8,8,256]{3,2,1,0:T(8,128)(2,1)S(1)} async-done(((bf16[16,8,8,256]{3,2,1,0:T(8,128)(2,1)}), bf16[16,8,8,256]{3,2,1,0:T(8,128)(2,1)S(1)}, u32[]{:S(2)}, u32[]{:S(2)}) %all-to-all-start.2) | async-done | bytes 524320 | tf_op jit(solution)/shard_map/all_to_all | solution.py:582
  200.0 15.9 %all_to_all.20 = bf16[16,8,8,256]{3,2,1,0:T(8,128)(2,1)S(1)} all-to-all(bf16[16,8,8,256]{3,2,1,0:T(8,128)(2,1)} %column_attention.3), channel_id=1, replica_groups=mesh['seq'=16,'res'=8] {'seq'}, dimensions={0} | all-to-all | bytes 1048576 | tf_op jit(solution)/shard_map/all_to_all | solution.py:582
  215.9 0.1 maximum_bitcast_fusion
  216.0 1.1 copy.54
  (15 shorter events, 0.0 us)
Async XLA Ops:
  0.6 8.3 %copy-start.10 = (bf16[128,8]{0,1:T(8,128)(2,1)S(1)}, bf16[128,8]{0,1:T(8,128)(2,1)}, u32[]{:S(2)}) copy-start(bf16[128,8]{0,1:T(8,128)(2,1)} %param.17) | copy-start | bytes 6148
  3.8 29.6 %collective-permute-start.2 = (bf16[8,256,256]{2,1,0:T(8,128)(2,1)}, bf16[8,256,256]{2,1,0:T(8,128)(2,1)}, u32[]{:S(2)}, u32[]{:S(2)}) collective-permute-start(bf16[8,256,256]{2,1,0:T(8,128)(2,1)} %norm_rows.1.refs_0_.rest_0_), channel_id=1, source_target_pairs={{4,0},{5,1},{6,2},{7,3},{0,4},{1,5},{2,6},{3,7},{12,8},{13,9},{14,... | collective-permute-start | bytes 3145736 | tf_op jit(solution)/shard_map/ppermute | solution.py:463
  6.3 29.8 %collective-permute-start.1 = (bf16[8,256,256]{2,1,0:T(8,128)(2,1)}, bf16[8,256,256]{2,1,0:T(8,128)(2,1)}, u32[]{:S(2)}, u32[]{:S(2)}) collective-permute-start(bf16[8,256,256]{2,1,0:T(8,128)(2,1)} %norm_rows.1.refs_0_.rest_0_), channel_id=1, source_target_pairs={{3,0},{0,1},{1,2},{2,3},{7,4},{4,5},{5,6},{6,7},{11,8},{8,9},{9,10... | collective-permute-start | bytes 3145736 | tf_op jit(solution)/shard_map/ppermute | solution.py:463
  7.5 28.6 %collective-permute-start = (bf16[8,256,256]{2,1,0:T(8,128)(2,1)}, bf16[8,256,256]{2,1,0:T(8,128)(2,1)}, u32[]{:S(2)}, u32[]{:S(2)}) collective-permute-start(bf16[8,256,256]{2,1,0:T(8,128)(2,1)} %norm_rows.1.refs_0_.rest_0_), channel_id=1, source_target_pairs={{1,0},{2,1},{3,2},{0,3},{5,4},{6,5},{7,6},{4,7},{9,8},{10,9},{11,1... | collective-permute-start | bytes 3145736 | tf_op jit(solution)/shard_map/ppermute | solution.py:463
  19.9 12.8 %copy-start = (bf16[8,256,128]{2,1,0:T(8,128)(2,1)S(1)}, bf16[8,256,128]{2,1,0:T(8,128)(2,1)}, u32[]{:S(2)}) copy-start(bf16[8,256,128]{2,1,0:T(8,128)(2,1)} %pair_bias.1.refs_13_) | copy-start | bytes 1572868
  19.9 12.7 %collective-permute-start.5 = (bf16[8,256,128]{2,1,0:T(8,128)(2,1)}, bf16[8,256,128]{2,1,0:T(8,128)(2,1)S(1)}, u32[]{:S(2)}, u32[]{:S(2)}) collective-permute-start(bf16[8,256,128]{2,1,0:T(8,128)(2,1)} %pair_bias.1.refs_13_), channel_id=1, source_target_pairs={{32,0},{40,8},{48,16},{56,24},{64,32},{72,40},{80,48},{88,56},{96,... | collective-permute-start | bytes 1572872 | tf_op jit(solution)/shard_map/ppermute | solution.py:456
  22.7 33.4 %collective-permute-start.7 = (bf16[8,256,128]{2,1,0:T(8,128)(2,1)}, bf16[8,256,128]{2,1,0:T(8,128)(2,1)S(1)}, u32[]{:S(2)}, u32[]{:S(2)}) collective-permute-start(bf16[8,256,128]{2,1,0:T(8,128)(2,1)} %pair_bias.1.refs_13_), channel_id=1, source_target_pairs={{16,0},{24,8},{0,16},{8,24},{48,32},{56,40},{32,48},{40,56},{80,64... | collective-permute-start | bytes 1572872 | tf_op jit(solution)/shard_map/ppermute | solution.py:456
  32.7 3.4 %copy-start.1 = (bf16[8,256,128]{2,1,0:T(8,128)(2,1)}, bf16[8,256,128]{2,1,0:T(8,128)(2,1)S(1)}, u32[]{:S(2)}) copy-start(bf16[8,256,128]{2,1,0:T(8,128)(2,1)S(1)} %collective-permute-done.5.refs_14_) | copy-start | bytes 1572868
  32.7 23.4 %collective-permute-start.6 = (bf16[8,256,128]{2,1,0:T(8,128)(2,1)S(1)}, bf16[8,256,128]{2,1,0:T(8,128)(2,1)S(1)}, u32[]{:S(2)}, u32[]{:S(2)}) collective-permute-start(bf16[8,256,128]{2,1,0:T(8,128)(2,1)S(1)} %copy-done), channel_id=1, source_target_pairs={{96,0},{104,8},{112,16},{120,24},{0,32},{8,40},{16,48},{24,56},{32... | collective-permute-start | bytes 1572872 | tf_op jit(solution)/shard_map/ppermute | solution.py:456
  33.4 22.7 %collective-permute-start.8 = (bf16[8,256,128]{2,1,0:T(8,128)(2,1)S(1)}, bf16[8,256,128]{2,1,0:T(8,128)(2,1)S(1)}, u32[]{:S(2)}, u32[]{:S(2)}) collective-permute-start(bf16[8,256,128]{2,1,0:T(8,128)(2,1)S(1)} %collective-permute-done.5.refs_14_), channel_id=1, source_target_pairs={{32,0},{40,8},{48,16},{56,24},{64,32},{72,40},{80,48},{88,56},{96,... | collective-permute-start | bytes 1572872 | tf_op jit(solution)/shard_map/ppermute | solution.py:456
  36.1 23.5 %collective-permute-start.4 = (bf16[8,256,256]{2,1,0:T(8,128)(2,1)}, bf16[8,256,256]{2,1,0:T(8,128)(2,1)}, u32[]{:S(2)}, u32[]{:S(2)}) collective-permute-start(bf16[8,256,256]{2,1,0:T(8,128)(2,1)} %get-tuple-element.54.refs_2_), channel_id=1, source_target_pairs={{3,0},{0,1},{1,2},{2,3},{7,4},{4,5},{5,6},{6,7},{11,8},{8,9},{9,10... | collective-permute-start | bytes 3145736 | tf_op jit(solution)/shard_map/ppermute | solution.py:463
  36.2 23.4 %collective-permute-start.3 = (bf16[8,256,256]{2,1,0:T(8,128)(2,1)}, bf16[8,256,256]{2,1,0:T(8,128)(2,1)}, u32[]{:S(2)}, u32[]{:S(2)}) collective-permute-start(bf16[8,256,256]{2,1,0:T(8,128)(2,1)} %get-tuple-element.55.refs_3_), channel_id=1, source_target_pairs={{1,0},{2,1},{3,2},{0,3},{5,4},{6,5},{7,6},{4,7},{9,8},{10,9},{11,1... | collective-permute-start | bytes 3145736 | tf_op jit(solution)/shard_map/ppermute | solution.py:463
  56.1 3.5 %copy-start.2 = (bf16[8,256,128]{2,1,0:T(8,128)(2,1)}, bf16[8,256,128]{2,1,0:T(8,128)(2,1)S(1)}, u32[]{:S(2)}) copy-start(bf16[8,256,128]{2,1,0:T(8,128)(2,1)S(1)} %collective-permute-done.7.refs_16_) | copy-start | bytes 1572868
  56.1 3.5 %copy-start.3 = (bf16[8,256,128]{2,1,0:T(8,128)(2,1)}, bf16[8,256,128]{2,1,0:T(8,128)(2,1)S(1)}, u32[]{:S(2)}) copy-start(bf16[8,256,128]{2,1,0:T(8,128)(2,1)S(1)} %collective-permute-done.6.refs_15_) | copy-start | bytes 1572868
  56.1 3.5 %copy-start.4 = (bf16[8,256,128]{2,1,0:T(8,128)(2,1)}, bf16[8,256,128]{2,1,0:T(8,128)(2,1)S(1)}, u32[]{:S(2)}) copy-start(bf16[8,256,128]{2,1,0:T(8,128)(2,1)S(1)} %collective-permute-done.8.refs_17_) | copy-start | bytes 1572868
  60.8 12.2 %collective-permute-start.13 = (bf16[8,256,128]{2,1,0:T(8,128)(2,1)}, bf16[8,256,128]{2,1,0:T(8,128)(2,1)S(1)}, u32[]{:S(2)}, u32[]{:S(2)}) collective-permute-start(bf16[8,256,128]{2,1,0:T(8,128)(2,1)} %get-tuple-element.91.refs_4_), channel_id=1, source_target_pairs={{16,0},{24,8},{0,16},{8,24},{48,32},{56,40},{32,48},{40,56},{80,64... | collective-permute-start | bytes 1572872 | tf_op jit(solution)/shard_map/ppermute | solution.py:456
  64.2 10.9 %collective-permute-start.12 = (bf16[8,256,128]{2,1,0:T(8,128)(2,1)}, bf16[8,256,128]{2,1,0:T(8,128)(2,1)S(1)}, u32[]{:S(2)}, u32[]{:S(2)}) collective-permute-start(bf16[8,256,128]{2,1,0:T(8,128)(2,1)} %get-tuple-element.90.refs_3_), channel_id=1, source_target_pairs={{96,0},{104,8},{112,16},{120,24},{0,32},{8,40},{16,48},{24,56},{32... | collective-permute-start | bytes 1572872 | tf_op jit(solution)/shard_map/ppermute | solution.py:456
  64.2 10.9 %collective-permute-start.11 = (bf16[8,256,128]{2,1,0:T(8,128)(2,1)}, bf16[8,256,128]{2,1,0:T(8,128)(2,1)S(1)}, u32[]{:S(2)}, u32[]{:S(2)}) collective-permute-start(bf16[8,256,128]{2,1,0:T(8,128)(2,1)} %get-tuple-element.90.refs_3_), channel_id=1, source_target_pairs={{32,0},{40,8},{48,16},{56,24},{64,32},{72,40},{80,48},{88,56},{96,... | collective-permute-start | bytes 1572872 | tf_op jit(solution)/shard_map/ppermute | solution.py:456
  66.9 25.5 %collective-permute-start.10 = (bf16[8,256,256]{2,1,0:T(8,128)(2,1)}, bf16[8,256,256]{2,1,0:T(8,128)(2,1)S(1)}, u32[]{:S(2)}, u32[]{:S(2)}) collective-permute-start(bf16[8,256,256]{2,1,0:T(8,128)(2,1)} %get-tuple-element.68.refs_3_), channel_id=1, source_target_pairs={{3,0},{0,1},{1,2},{2,3},{7,4},{4,5},{5,6},{6,7},{11,8},{8,9},{9,10... | collective-permute-start | bytes 3145736 | tf_op jit(solution)/shard_map/ppermute | solution.py:463
  66.9 25.5 %collective-permute-start.9 = (bf16[8,256,256]{2,1,0:T(8,128)(2,1)}, bf16[8,256,256]{2,1,0:T(8,128)(2,1)}, u32[]{:S(2)}, u32[]{:S(2)}) collective-permute-start(bf16[8,256,256]{2,1,0:T(8,128)(2,1)} %get-tuple-element.69.refs_0_.refs_4_), channel_id=1, source_target_pairs={{1,0},{2,1},{3,2},{0,3},{5,4},{6,5},{7,6},{4,7},{9,8},{10,9},{11,1... | collective-permute-start | bytes 3145736 | tf_op jit(solution)/shard_map/ppermute | solution.py:463
  73.0 2.1 copy-start.5
  75.1 0.8 copy-start.6
  75.1 1.0 copy-start.7
  80.9 12.4 %collective-permute-start.14 = (bf16[8,8,256,128]{3,2,1,0:T(8,128)(2,1)}, bf16[8,8,256,128]{3,2,1,0:T(8,128)(2,1)}, u32[]{:S(2)}, u32[]{:S(2)}) collective-permute-start(bf16[8,8,256,128]{3,2,1,0:T(8,128)(2,1)} %pack_blocks.1.refs_14_), channel_id=1, source_target_pairs={{8,0},{0,8},{24,16},{16,24},{40,32},{32,40},{56,48},{48,56},{72,64... | collective-permute-start | bytes 12582920 | tf_op jit(solution)/shard_map/ppermute | solution.py:456
  92.3 1.0 copy-start.11
  126.5 38.1 %all-to-all-start.1 = ((bf16[16,8,8,256]{3,2,1,0:T(8,128)(2,1)}), bf16[16,8,8,256]{3,2,1,0:T(8,128)(2,1)S(1)}, u32[]{:S(2)}, u32[]{:S(2)}) async-start(bf16[16,8,8,256]{3,2,1,0:T(8,128)(2,1)} %get-tuple-element.98), calls=%async_computation.1 | async-start | bytes 1048576 | tf_op jit(solution)/shard_map/all_to_all | solution.py:578
  164.7 7.3 %copy-start.8 = (bf16[16,8,8,256]{3,2,1,0:T(8,128)(2,1)}, bf16[16,8,8,256]{3,2,1,0:T(8,128)(2,1)S(1)}, u32[]{:S(2)}) copy-start(bf16[16,8,8,256]{3,2,1,0:T(8,128)(2,1)S(1)} %all-to-all-done.1.x_ref) | copy-start | bytes 1572868
  164.7 18.4 %all-to-all-start = ((bf16[16,8,8,256]{3,2,1,0:T(8,128)(2,1)}), bf16[16,8,8,256]{3,2,1,0:T(8,128)(2,1)S(1)}, u32[]{:S(2)}, u32[]{:S(2)}) async-start(bf16[16,8,8,256]{3,2,1,0:T(8,128)(2,1)} %get-tuple-element.97), calls=%async_computation | async-start | bytes 1048576 | tf_op jit(solution)/shard_map/all_to_all | solution.py:578
  183.1 0.8 copy-start.9
  183.9 16.1 %all-to-all-start.2 = ((bf16[16,8,8,256]{3,2,1,0:T(8,128)(2,1)}), bf16[16,8,8,256]{3,2,1,0:T(8,128)(2,1)S(1)}, u32[]{:S(2)}, u32[]{:S(2)}) async-start(bf16[16,8,8,256]{3,2,1,0:T(8,128)(2,1)} %get-tuple-element.100), calls=%async_computation.2 | async-start | bytes 1048576 | tf_op jit(solution)/shard_map/all_to_all | solution.py:582

commit v3 on v2

--- a/solution.py
+++ b/solution.py
@@ -201,14 +201,13 @@
 
 
 def row_kernel(spec, *refs):
-    n_skip, turn, offsets, n_values, places = spec
+    offsets, n_values, places = spec
     n_keys = len(offsets)
     refs = list(refs)
     take = lambda n: [refs.pop(0) for _ in range(n)]
     keys, values = take(n_keys), take(n_values)
     bias_in = take(len(places))
     q_ref, gate_ref, emb_ref, fast_ref, wv_ref, wm_ref = take(6)
-    take(n_skip)
     out_ref, send_ref, bias, late, sems = refs
     each, block, width = keys[0].shape
     _, heads, rows, tile = bias.shape
@@ -219,7 +218,6 @@
     res = lax.axis_index("res")
 
     def copies():
-        here = pl.ds(turn * rows, rows)
         n = 0
         for ref, group in zip(bias_in, places):
             for i, (dy, dz, dc) in enumerate(group):
@@ -228,7 +226,7 @@
                     + lax.rem(seq // 2 + dz, 2) * 2
                     + lax.rem(seq + dc, 2)
                 )
-                yield pltpu.make_async_copy(ref.at[i, :, here], bias.at[place], sems.at[n])
+                yield pltpu.make_async_copy(ref.at[i], bias.at[place], sems.at[n])
                 n += 1
 
     @pl.when(first)
@@ -303,33 +301,26 @@
         lax.fori_loop(0, each, lambda i, carry: (mix(i, True), carry)[1], 0)
 
 
-def row_attention(keys, values, bias, queries, gate, fast, emb, wv, wm, turn, rows_done=None):
+def row_attention(keys, values, bias, queries, gate, fast, emb, wv, wm):
     offsets, places = tuple(keys), tuple(bias)
     seqs, block, width = emb.shape
-    _, heads, block, tile = bias[places[0]].shape
+    _, heads, rows, tile = bias[places[0]].shape
     tiles = sum(len(group) for group in places)
-    rows = block // 2
     parts = lax.axis_size("seq")
     part = rows // parts
     each = 1
-    mine = pl.BlockSpec((each, rows, width), lambda s: (s, turn, 0))
+    mine = pl.BlockSpec((each, rows, width), lambda s: (s, 0, 0))
     args = [*keys.values(), *values, *bias.values(), queries, gate, emb, fast, wv, wm]
     specs = [pl.BlockSpec((each, block, width), lambda s: (s, 0, 0))] * (len(keys) + len(values))
     specs += [pl.BlockSpec(memory_space=pl.ANY)] * len(bias)
-    specs += [pl.BlockSpec((each, heads, rows, width), lambda s: (s, 0, turn, 0)), mine, mine]
+    specs += [pl.BlockSpec((each, heads, rows, width), lambda s: (s, 0, 0, 0)), mine, mine]
     specs += [pl.BlockSpec(memory_space=pltpu.SMEM), right_half(wv), whole(*wm.shape)]
-    aliases = {}
-    skipped = []
-    if rows_done is not None:
-        aliases[len(args)] = 0
-        skipped.append(rows_done)
-    skip_args, skip_specs = after(*skipped)
-    spec = (len(skipped), turn, offsets, len(values), places)
+    spec = (offsets, len(values), places)
     return pl.pallas_call(
         functools.partial(row_kernel, spec),
         grid=(seqs // each,),
         name="row_attention",
-        in_specs=specs + skip_specs,
+        in_specs=specs,
         out_specs=[mine, pl.BlockSpec((parts, each, part, width), lambda s: (0, s, 0, 0))],
         out_shape=[
             jax.ShapeDtypeStruct(emb.shape, BF16),
@@ -340,10 +331,9 @@
             pltpu.VMEM((each, len(keys) - len(values), block, width), BF16),
             pltpu.SemaphoreType.DMA((tiles,)),
         ],
-        input_output_aliases=aliases,
         compiler_params=pltpu.CompilerParams(vmem_limit_bytes=VMEM_LIMIT),
-        cost_estimate=cost(22),
-    )(*args, *skip_args)
+        cost_estimate=cost(45),
+    )(*args)
 
 
 def column_kernel(
@@ -566,22 +556,17 @@
     keys = {o: a[o] for o in order}
     rest = ([*early, *middle], bias, *queries, homolog_embedding, lookup)
     rest += (horizontal_merge_weights,)
-    after_rows, send_0 = row_attention(keys, *rest, 0)
-    after_rows, send_1 = row_attention(keys, *rest, 1, after_rows)
-    column = (
+    after_rows, send = row_attention(keys, *rest)
+    result = column_attention(
+        lax.all_to_all(send, "seq", 0, 0, tiled=True),
         sequence_key_mask,
         cqk,
         vertical_lookup_weights,
         vertical_sigmoid_weights,
         vertical_merge_weights,
     )
-    x_0, x_1 = (lax.all_to_all(x, "seq", 0, 0, tiled=True) for x in (send_0, send_1))
-    done_0 = column_attention(x_0, *column, (after_rows,))
-    x_1, done_0 = hold(x_1, done_0)
-    done_1 = column_attention(x_1, *column)
-    finals = [lax.all_to_all(x, "seq", 0, 0, tiled=True) for x in (done_0, done_1)]
-    final = jnp.transpose(jnp.stack(finals), (2, 0, 1, 3, 4)).reshape(seqs, res, width)
-    return after_rows, final
+    back = lax.all_to_all(result, "seq", 0, 0, tiled=True)
+    return after_rows, jnp.transpose(back, (1, 0, 2, 3)).reshape(seqs, res, width)
 
 
 def solution(mesh):

time: 218 us -> 206 us (0.945)
  blocking collectives: 15.9 us -> 42.6 us
  starting transfers between devices: 48 us -> 30.9 us
  Pallas kernels: 129 us -> 113 us
  waiting for transfers between devices: 19 us -> 12.8 us
    all_to_all x1 -> x2, blocking collectives: 15.9 us -> 42.6 us  [the longest x1 21.6 us: per_device(): back = lax.all_to_all(result, 'seq', 0, 0, tiled=True)]
    all_to_all x3 -> x0, starting transfers between devices: 17.1 us -> none  [per_device(): lax.all_to_all(x, 'seq', 0, 0, tiled=True)]
    pallas_call x2 -> x1, Pallas kernels: 66.4 us -> 52.8 us  [row_attention(): pl.pallas_call(functools.partial(row_kernel, spec), grid=(seqs // each,),...]
    all_to_all x3 -> x0, waiting for transfers between devices: 6.3 us -> none  [per_device(): lax.all_to_all(x, 'seq', 0, 0, tiled=True)]
    pallas_call x2 -> x1, Pallas kernels: 16 us -> 13.9 us  [column_attention(): pl.pallas_call(column_kernel, grid=(1,), name='column_attention', in_spec...]
  transfers between devices with their start and end apart: 18 -> 15, of which waited for: 6 -> 4; matrix products, arithmetic and copies ran while one was open for 0% -> 0% of each run, Pallas kernels for 42% -> 21%
where the time goes in v3:
time: 206 us; the launch traced here: 204 us
  Pallas kernels  113 us (55%)
  blocking collectives  42.6 us (21%)
  starting transfers between devices  30.9 us (15%)
  waiting for transfers between devices  12.8 us (6%)
  local copies, waits for them, and re-layouts  3.82 us (2%)
    pallas_call x1, Pallas kernels, row_attention(): pl.pallas_call(functools.partial(row_kernel, spec), grid=(seqs // each,),...  52.8 us
    all_to_all x1, blocking collectives, per_device(): back = lax.all_to_all(result, 'seq', 0, 0, tiled=True)  21.6 us
    all_to_all x1, blocking collectives, per_device(): lax.all_to_all(send, 'seq', 0, 0, tiled=True)  21 us
    ppermute x8, starting transfers between devices, fetch_seq(): return lax.ppermute(x, 'seq', pairs)  20.3 us
    pallas_call x2, Pallas kernels, row_values(): pl.pallas_call(value_kernel, grid=(seqs,), name='row_values', in_specs=[o...  14.2 us
    pallas_call x1, Pallas kernels, column_attention(): pl.pallas_call(column_kernel, grid=(1,), name='column_attention', in_spec...  13.9 us
    ppermute x7, starting transfers between devices, fetch_row(): return lax.ppermute(x, 'res', pairs)  10.6 us
    pallas_call x1, Pallas kernels, pair_bias(): pl.pallas_call(pair_kernel, grid=(rows // step,), name='pair_bias', in_sp...  10.2 us
  transfers between devices with their start and end apart: 15, of which 4 were waited for; matrix products, arithmetic and copies ran while one was open for 0% of the time, Pallas kernels for 21%

profile of v3, /device:TPU:1, one launch (start us, length us, event | category | flops | bytes accessed | tf_op | source)
XLA Modules:
  0.0 203.7 jit_solution(3372358163635978005)
XLA Ops:
  0.6 0.0 copy-start.8
  0.6 3.2 %norm_rows.1.refs_0_.rest_0_ = bf16[8,256,256]{2,1,0:T(8,128)(2,1)} custom-call(bf16[8,256,256]{2,1,0:T(8,128)(2,1)} %refs_18_.1), custom_call_target="tpu_custom_call" | custom-call | flops 2000000000 | tf_op jit(solution)/shard_map/norm_rows/pallas_call | solution.py:54
  3.8 2.5 %collective-permute-start.2 = (bf16[8,256,256]{2,1,0:T(8,128)(2,1)}, bf16[8,256,256]{2,1,0:T(8,128)(2,1)}, u32[]{:S(2)}, u32[]{:S(2)}) collective-permute-start(bf16[8,256,256]{2,1,0:T(8,128)(2,1)} %norm_rows.1.refs_0_.rest_0_), channel_id=1, source_target_pairs={{4,0},{5,1},{6,2},{7,3},{0,4},{1,5},{2,6},{3,7},{12,8},{13,9},{14,... | collective-permute-start | bytes 3145736 | tf_op jit(solution)/shard_map/ppermute | solution.py:453
  6.3 1.2 collective-permute-start.1
  7.5 1.5 collective-permute-start
  9.0 0.0 copy-done.8
  9.0 0.7 copy.49.head_ref.w_ref
  9.7 10.2 %pair_bias.1.refs_13_ = bf16[8,256,128]{2,1,0:T(8,128)(2,1)} custom-call(bf16[256,128,128]{2,1,0:T(8,128)(2,1)} %x_ref.3, bf16[128,8]{1,0:T(8,128)(2,1)} %copy.49.head_ref.w_ref, s32[16,128]{1,0:T(8,128)} %bitcast.6, bf16[8,256,256]{2,1,0:T(8,128)(2,1)} %norm_rows.1.refs_0_.rest_0_), custom_call_target="tpu_custom_call" | custom-call | flops 6000000000 | tf_op jit(solution)/shard_map/pair_bias/pallas_call | solution.py:115
  19.9 0.0 copy-start
  19.9 2.7 %collective-permute-start.5 = (bf16[8,256,128]{2,1,0:T(8,128)(2,1)}, bf16[8,256,128]{2,1,0:T(8,128)(2,1)S(1)}, u32[]{:S(2)}, u32[]{:S(2)}) collective-permute-start(bf16[8,256,128]{2,1,0:T(8,128)(2,1)} %pair_bias.1.refs_13_), channel_id=1, source_target_pairs={{32,0},{40,8},{48,16},{56,24},{64,32},{72,40},{80,48},{88,56},{96,... | collective-permute-start | bytes 1572872 | tf_op jit(solution)/shard_map/ppermute | solution.py:446
  22.6 3.3 %collective-permute-start.7 = (bf16[8,256,128]{2,1,0:T(8,128)(2,1)}, bf16[8,256,128]{2,1,0:T(8,128)(2,1)S(1)}, u32[]{:S(2)}, u32[]{:S(2)}) collective-permute-start(bf16[8,256,128]{2,1,0:T(8,128)(2,1)} %pair_bias.1.refs_13_), channel_id=1, source_target_pairs={{16,0},{24,8},{0,16},{8,24},{48,32},{56,40},{32,48},{40,56},{80,64... | collective-permute-start | bytes 1572872 | tf_op jit(solution)/shard_map/ppermute | solution.py:446
  25.9 3.0 %fold_weights.1 = (bf16[256,2048]{1,0:T(8,128)(2,1)}, bf16[256,2048]{1,0:T(8,128)(2,1)}, f32[1]{0:T(128)}) custom-call(s32[16,128]{1,0:T(8,128)} %bitcast.7, bf16[128,8]{1,0:T(8,128)(2,1)} %copy.49.head_ref.w_ref, bf16[256,256]{1,0:T(8,128)(2,1)} %rq_ref.1, bf16[256,512]{1,0:T(8,128)(2,1)} %refs_20_.1, bf16[256,256]{1,0:T(8,128)(2,1)} %cq_ref.1, ...), custom_call_target="tpu_custom_call" | custom-call | flops 3000000000 | tf_op jit(solution)/shard_map/fold_weights/pallas_call | solution.py:429
  29.0 3.7 %collective-permute-done.5.refs_14_ = bf16[8,256,128]{2,1,0:T(8,128)(2,1)S(1)} collective-permute-done((bf16[8,256,128]{2,1,0:T(8,128)(2,1)}, bf16[8,256,128]{2,1,0:T(8,128)(2,1)S(1)}, u32[]{:S(2)}, u32[]{:S(2)}) %collective-permute-start.5) | collective-permute-done | bytes 524320 | tf_op jit(solution)/shard_map/ppermute | solution.py:446
  32.7 0.0 copy-done
  32.7 0.0 copy-start.1
  32.7 0.8 collective-permute-start.6
  33.4 0.0 collective-permute-done.2.refs_3_
  33.4 2.6 %collective-permute-start.8 = (bf16[8,256,128]{2,1,0:T(8,128)(2,1)S(1)}, bf16[8,256,128]{2,1,0:T(8,128)(2,1)S(1)}, u32[]{:S(2)}, u32[]{:S(2)}) collective-permute-start(bf16[8,256,128]{2,1,0:T(8,128)(2,1)S(1)} %collective-permute-done.5.refs_14_), channel_id=1, source_target_pairs={{32,0},{40,8},{48,16},{56,24},{64,32},{72,40},{80,48},{88,56},{96,... | collective-permute-start | bytes 1572872 | tf_op jit(solution)/shard_map/ppermute | solution.py:446
  36.1 0.0 collective-permute-done.1.refs_2_
  36.1 0.0 collective-permute-done.refs_1_
  36.1 0.0 copy-done.1
  36.1 0.1 collective-permute-start.4
  36.2 2.7 %collective-permute-start.3 = (bf16[8,256,256]{2,1,0:T(8,128)(2,1)}, bf16[8,256,256]{2,1,0:T(8,128)(2,1)}, u32[]{:S(2)}, u32[]{:S(2)}) collective-permute-start(bf16[8,256,256]{2,1,0:T(8,128)(2,1)} %get-tuple-element.51.refs_3_), channel_id=1, source_target_pairs={{1,0},{2,1},{3,2},{0,3},{5,4},{6,5},{7,6},{4,7},{9,8},{10,9},{11,1... | collective-permute-start | bytes 3145736 | tf_op jit(solution)/shard_map/ppermute | solution.py:453
  38.8 7.6 %row_values.2 = (bf16[8,256,256]{2,1,0:T(8,128)(2,1)}, bf16[8,256,256]{2,1,0:T(8,128)(2,1)}, bf16[8,256,256]{2,1,0:T(8,128)(2,1)}, bf16[8,256,256]{2,1,0:T(8,128)(2,1)}) custom-call(bf16[8,256,256]{2,1,0:T(8,128)(2,1)} %get-tuple-element.48.refs_0_.own_ref, bf16[8,256,256]{2,1,0:T(8,128)(2,1)} %get-tuple-element.49.refs_1_, ...), custom_call_target="tpu_custom_call" | custom-call | flops 6000000000 | tf_op jit(solution)/shard_map/row_values/pallas_call | solution.py:192
  46.4 9.6 %row_queries.1 = (bf16[8,8,256,256]{3,2,1,0:T(8,128)(2,1)}, f32[8,256,256]{2,1,0:T(8,128)}, s32[1]{0:T(128)}) custom-call(bf16[8,256,256]{2,1,0:T(8,128)(2,1)} %get-tuple-element.48.refs_0_.own_ref, bf16[256,2048]{1,0:T(8,128)(2,1)} %get-tuple-element.56.wqk_ref, bf16[256,256]{1,0:T(8,128)(2,1)} %wg_ref.2, f32[1]{0:T(128)} %get-tuple-element.57.limit_ref), custom_call_target="tpu_custom_call" | custom-call | flops 6000000000 | tf_op jit(solution)/shard_map/row_queries/pallas_call | solution.py:159
  56.0 0.0 collective-permute-done.7.refs_16_
  56.0 0.0 copy-start.2
  56.0 0.0 collective-permute-done.6.refs_15_
  56.0 0.0 copy-start.3
  56.0 0.0 collective-permute-done.8.refs_17_
  56.0 0.0 copy-start.4
  56.1 3.5 %collective-permute-done.4.refs_5_ = bf16[8,256,256]{2,1,0:T(8,128)(2,1)} collective-permute-done((bf16[8,256,256]{2,1,0:T(8,128)(2,1)}, bf16[8,256,256]{2,1,0:T(8,128)(2,1)}, u32[]{:S(2)}, u32[]{:S(2)}) %collective-permute-start.4) | collective-permute-done | bytes 1048608 | tf_op jit(solution)/shard_map/ppermute | solution.py:453
  59.6 0.0 collective-permute-done.3.refs_4_
  59.6 0.0 copy-done.2
  59.6 0.0 copy-done.3
  59.6 0.0 copy-done.4
  59.6 1.1 step_done.4
  60.8 3.4 %collective-permute-start.13 = (bf16[8,256,128]{2,1,0:T(8,128)(2,1)}, bf16[8,256,128]{2,1,0:T(8,128)(2,1)S(1)}, u32[]{:S(2)}, u32[]{:S(2)}) collective-permute-start(bf16[8,256,128]{2,1,0:T(8,128)(2,1)} %get-tuple-element.87.refs_4_), channel_id=1, source_target_pairs={{16,0},{24,8},{0,16},{8,24},{48,32},{56,40},{32,48},{40,56},{80,64... | collective-permute-start | bytes 1572872 | tf_op jit(solution)/shard_map/ppermute | solution.py:446
  64.1 0.0 collective-permute-start.12
  64.2 2.7 %collective-permute-start.11 = (bf16[8,256,128]{2,1,0:T(8,128)(2,1)}, bf16[8,256,128]{2,1,0:T(8,128)(2,1)S(1)}, u32[]{:S(2)}, u32[]{:S(2)}) collective-permute-start(bf16[8,256,128]{2,1,0:T(8,128)(2,1)} %get-tuple-element.86.refs_3_), channel_id=1, source_target_pairs={{32,0},{40,8},{48,16},{56,24},{64,32},{72,40},{80,48},{88,56},{96,... | collective-permute-start | bytes 1572872 | tf_op jit(solution)/shard_map/ppermute | solution.py:446
  66.8 0.0 collective-permute-start.10
  66.8 2.7 %collective-permute-start.9 = (bf16[8,256,256]{2,1,0:T(8,128)(2,1)}, bf16[8,256,256]{2,1,0:T(8,128)(2,1)}, u32[]{:S(2)}, u32[]{:S(2)}) collective-permute-start(bf16[8,256,256]{2,1,0:T(8,128)(2,1)} %get-tuple-element.65.refs_0_.refs_4_), channel_id=1, source_target_pairs={{1,0},{2,1},{3,2},{0,3},{5,4},{6,5},{7,6},{4,7},{9,8},{10,9},{11,1... | collective-permute-start | bytes 3145736 | tf_op jit(solution)/shard_map/ppermute | solution.py:453
  69.5 3.4 %collective-permute-done.13.refs_7_ = bf16[8,256,128]{2,1,0:T(8,128)(2,1)S(1)} collective-permute-done((bf16[8,256,128]{2,1,0:T(8,128)(2,1)}, bf16[8,256,128]{2,1,0:T(8,128)(2,1)S(1)}, u32[]{:S(2)}, u32[]{:S(2)}) %collective-permute-start.13) | collective-permute-done | bytes 524320 | tf_op jit(solution)/shard_map/ppermute | solution.py:446
  73.0 0.0 copy-start.5
  73.0 2.1 %collective-permute-done.12.refs_6_ = bf16[8,256,128]{2,1,0:T(8,128)(2,1)S(1)} collective-permute-done((bf16[8,256,128]{2,1,0:T(8,128)(2,1)}, bf16[8,256,128]{2,1,0:T(8,128)(2,1)S(1)}, u32[]{:S(2)}, u32[]{:S(2)}) %collective-permute-start.12) | collective-permute-done | bytes 524320 | tf_op jit(solution)/shard_map/ppermute | solution.py:446
  75.1 0.0 copy-start.6
  75.1 0.0 collective-permute-done.11.refs_5_
  75.1 0.0 copy-start.7
  75.1 0.0 copy-done.5
  75.1 0.8 copy-done.6
  75.9 0.2 copy-done.7
  76.1 4.8 %pack_blocks.1.refs_14_ = bf16[8,8,256,128]{3,2,1,0:T(8,128)(2,1)} custom-call(bf16[8,256,128]{2,1,0:T(8,128)(2,1)} %get-tuple-element.83.refs_0_, bf16[8,256,128]{2,1,0:T(8,128)(2,1)} %get-tuple-element.84.refs_1_, bf16[8,256,128]{2,1,0:T(8,128)(2,1)} %get-tuple-element.85.refs_2_, bf16[8,256,128]{2,1,0:T(8,128)(2,1)} %get-tuple-element.86.refs_3_, ...), custom_call_target="tpu_custom_call" | custom-call | flops 2000000000 | tf_op jit(solution)/shard_map/pack_blocks/pallas_call | solution.py:464
  80.9 4.8 %collective-permute-start.14 = (bf16[8,8,256,128]{3,2,1,0:T(8,128)(2,1)}, bf16[8,8,256,128]{3,2,1,0:T(8,128)(2,1)}, u32[]{:S(2)}, u32[]{:S(2)}) collective-permute-start(bf16[8,8,256,128]{3,2,1,0:T(8,128)(2,1)} %pack_blocks.1.refs_14_), channel_id=1, source_target_pairs={{8,0},{0,8},{24,16},{16,24},{40,32},{32,40},{56,48},{48,56},{72,64... | collective-permute-start | bytes 12582920 | tf_op jit(solution)/shard_map/ppermute | solution.py:446
  85.7 6.6 %row_values.3 = (bf16[8,256,256]{2,1,0:T(8,128)(2,1)}, bf16[8,256,256]{2,1,0:T(8,128)(2,1)}) custom-call(bf16[8,256,256]{2,1,0:T(8,128)(2,1)} %get-tuple-element.65.refs_0_.refs_4_, bf16[8,256,256]{2,1,0:T(8,128)(2,1)} %get-tuple-element.66.refs_1_.refs_5_, bf16[256,512]{1,0:T(8,128)(2,1)} %refs_20_.1), custom_call_target="tpu_custom_call" | custom-call | flops 3000000000 | tf_op jit(solution)/shard_map/row_values/pallas_call | solution.py:192
  92.3 0.0 collective-permute-done.10.refs_7_
  92.3 0.0 copy-start.9
  92.3 0.0 collective-permute-done.9.refs_6_
  92.3 1.0 copy-done.9
  93.3 0.0 collective-permute-done.14.refs_15_
  93.3 52.8 %row_attention.1 = (bf16[8,256,256]{2,1,0:T(8,128)(2,1)}, bf16[16,8,16,256]{3,2,1,0:T(8,128)(2,1)}) custom-call(bf16[8,256,256]{2,1,0:T(8,128)(2,1)} %get-tuple-element.69.refs_0_, bf16[8,256,256]{2,1,0:T(8,128)(2,1)} %get-tuple-element.70.refs_1_, bf16[8,256,256]{2,1,0:T(8,128)(2,1)} %get-tuple-element.71.refs_2_, ...), custom_call_target="tpu_custom_call" | custom-call | flops 44999999488 | tf_op jit(solution)/shard_map/row_attention/pallas_call | solution.py:319
  146.2 21.0 %all_to_all.10.x_ref = bf16[16,8,16,256]{3,2,1,0:T(8,128)(2,1)} all-to-all(bf16[16,8,16,256]{3,2,1,0:T(8,128)(2,1)} %get-tuple-element.92), channel_id=1, replica_groups=mesh['seq'=16,'res'=8] {'seq'}, dimensions={0} | all-to-all | bytes 2097152 | tf_op jit(solution)/shard_map/all_to_all | solution.py:561
  167.2 13.9 %column_attention.1 = bf16[16,8,16,256]{3,2,1,0:T(8,128)(2,1)} custom-call(bf16[16,8,16,256]{3,2,1,0:T(8,128)(2,1)} %all_to_all.10.x_ref, s32[1,128]{1,0:T(1,128)} %bitcast.8, bf16[256,2048]{1,0:T(8,128)(2,1)} %get-tuple-element.93.wqk_ref, bf16[256,512]{1,0:T(8,128)(2,1)} %wv_ref.1, bf16[256,256]{1,0:T(8,128)(2,1)} %wg_ref.3, bf16[256,256]{1,0:T(8,128)(2,1)} %wm_ref.1), custom_call_target="tpu_custom_call" | custom-call | flops 8000000000 | tf_op jit(solution)/shard_map/column_attention/pallas_call | solution.py:386
  181.1 21.6 %all_to_all.11 = bf16[16,8,16,256]{3,2,1,0:T(8,128)(2,1)S(1)} all-to-all(bf16[16,8,16,256]{3,2,1,0:T(8,128)(2,1)} %column_attention.1), channel_id=1, replica_groups=mesh['seq'=16,'res'=8] {'seq'}, dimensions={0} | all-to-all | bytes 2097152 | tf_op jit(solution)/shard_map/all_to_all | solution.py:568
  202.6 1.1 copy.51
  (2 shorter events, 0.0 us)
Async XLA Ops:
  0.6 8.3 %copy-start.8 = (bf16[128,8]{0,1:T(8,128)(2,1)S(1)}, bf16[128,8]{0,1:T(8,128)(2,1)}, u32[]{:S(2)}) copy-start(bf16[128,8]{0,1:T(8,128)(2,1)} %param.17) | copy-start | bytes 6148
  3.8 29.6 %collective-permute-start.2 = (bf16[8,256,256]{2,1,0:T(8,128)(2,1)}, bf16[8,256,256]{2,1,0:T(8,128)(2,1)}, u32[]{:S(2)}, u32[]{:S(2)}) collective-permute-start(bf16[8,256,256]{2,1,0:T(8,128)(2,1)} %norm_rows.1.refs_0_.rest_0_), channel_id=1, source_target_pairs={{4,0},{5,1},{6,2},{7,3},{0,4},{1,5},{2,6},{3,7},{12,8},{13,9},{14,... | collective-permute-start | bytes 3145736 | tf_op jit(solution)/shard_map/ppermute | solution.py:453
  6.3 29.8 %collective-permute-start.1 = (bf16[8,256,256]{2,1,0:T(8,128)(2,1)}, bf16[8,256,256]{2,1,0:T(8,128)(2,1)}, u32[]{:S(2)}, u32[]{:S(2)}) collective-permute-start(bf16[8,256,256]{2,1,0:T(8,128)(2,1)} %norm_rows.1.refs_0_.rest_0_), channel_id=1, source_target_pairs={{3,0},{0,1},{1,2},{2,3},{7,4},{4,5},{5,6},{6,7},{11,8},{8,9},{9,10... | collective-permute-start | bytes 3145736 | tf_op jit(solution)/shard_map/ppermute | solution.py:453
  7.5 28.6 %collective-permute-start = (bf16[8,256,256]{2,1,0:T(8,128)(2,1)}, bf16[8,256,256]{2,1,0:T(8,128)(2,1)}, u32[]{:S(2)}, u32[]{:S(2)}) collective-permute-start(bf16[8,256,256]{2,1,0:T(8,128)(2,1)} %norm_rows.1.refs_0_.rest_0_), channel_id=1, source_target_pairs={{1,0},{2,1},{3,2},{0,3},{5,4},{6,5},{7,6},{4,7},{9,8},{10,9},{11,1... | collective-permute-start | bytes 3145736 | tf_op jit(solution)/shard_map/ppermute | solution.py:453
  19.9 12.8 %copy-start = (bf16[8,256,128]{2,1,0:T(8,128)(2,1)S(1)}, bf16[8,256,128]{2,1,0:T(8,128)(2,1)}, u32[]{:S(2)}) copy-start(bf16[8,256,128]{2,1,0:T(8,128)(2,1)} %pair_bias.1.refs_13_) | copy-start | bytes 1572868
  19.9 12.8 %collective-permute-start.5 = (bf16[8,256,128]{2,1,0:T(8,128)(2,1)}, bf16[8,256,128]{2,1,0:T(8,128)(2,1)S(1)}, u32[]{:S(2)}, u32[]{:S(2)}) collective-permute-start(bf16[8,256,128]{2,1,0:T(8,128)(2,1)} %pair_bias.1.refs_13_), channel_id=1, source_target_pairs={{32,0},{40,8},{48,16},{56,24},{64,32},{72,40},{80,48},{88,56},{96,... | collective-permute-start | bytes 1572872 | tf_op jit(solution)/shard_map/ppermute | solution.py:446
  22.6 33.4 %collective-permute-start.7 = (bf16[8,256,128]{2,1,0:T(8,128)(2,1)}, bf16[8,256,128]{2,1,0:T(8,128)(2,1)S(1)}, u32[]{:S(2)}, u32[]{:S(2)}) collective-permute-start(bf16[8,256,128]{2,1,0:T(8,128)(2,1)} %pair_bias.1.refs_13_), channel_id=1, source_target_pairs={{16,0},{24,8},{0,16},{8,24},{48,32},{56,40},{32,48},{40,56},{80,64... | collective-permute-start | bytes 1572872 | tf_op jit(solution)/shard_map/ppermute | solution.py:446
  32.7 3.4 %copy-start.1 = (bf16[8,256,128]{2,1,0:T(8,128)(2,1)}, bf16[8,256,128]{2,1,0:T(8,128)(2,1)S(1)}, u32[]{:S(2)}) copy-start(bf16[8,256,128]{2,1,0:T(8,128)(2,1)S(1)} %collective-permute-done.5.refs_14_) | copy-start | bytes 1572868
  32.7 23.3 %collective-permute-start.6 = (bf16[8,256,128]{2,1,0:T(8,128)(2,1)S(1)}, bf16[8,256,128]{2,1,0:T(8,128)(2,1)S(1)}, u32[]{:S(2)}, u32[]{:S(2)}) collective-permute-start(bf16[8,256,128]{2,1,0:T(8,128)(2,1)S(1)} %copy-done), channel_id=1, source_target_pairs={{96,0},{104,8},{112,16},{120,24},{0,32},{8,40},{16,48},{24,56},{32... | collective-permute-start | bytes 1572872 | tf_op jit(solution)/shard_map/ppermute | solution.py:446
  33.4 22.6 %collective-permute-start.8 = (bf16[8,256,128]{2,1,0:T(8,128)(2,1)S(1)}, bf16[8,256,128]{2,1,0:T(8,128)(2,1)S(1)}, u32[]{:S(2)}, u32[]{:S(2)}) collective-permute-start(bf16[8,256,128]{2,1,0:T(8,128)(2,1)S(1)} %collective-permute-done.5.refs_14_), channel_id=1, source_target_pairs={{32,0},{40,8},{48,16},{56,24},{64,32},{72,40},{80,48},{88,56},{96,... | collective-permute-start | bytes 1572872 | tf_op jit(solution)/shard_map/ppermute | solution.py:446
  36.1 23.5 %collective-permute-start.4 = (bf16[8,256,256]{2,1,0:T(8,128)(2,1)}, bf16[8,256,256]{2,1,0:T(8,128)(2,1)}, u32[]{:S(2)}, u32[]{:S(2)}) collective-permute-start(bf16[8,256,256]{2,1,0:T(8,128)(2,1)} %get-tuple-element.50.refs_2_), channel_id=1, source_target_pairs={{3,0},{0,1},{1,2},{2,3},{7,4},{4,5},{5,6},{6,7},{11,8},{8,9},{9,10... | collective-permute-start | bytes 3145736 | tf_op jit(solution)/shard_map/ppermute | solution.py:453
  36.2 23.5 %collective-permute-start.3 = (bf16[8,256,256]{2,1,0:T(8,128)(2,1)}, bf16[8,256,256]{2,1,0:T(8,128)(2,1)}, u32[]{:S(2)}, u32[]{:S(2)}) collective-permute-start(bf16[8,256,256]{2,1,0:T(8,128)(2,1)} %get-tuple-element.51.refs_3_), channel_id=1, source_target_pairs={{1,0},{2,1},{3,2},{0,3},{5,4},{6,5},{7,6},{4,7},{9,8},{10,9},{11,1... | collective-permute-start | bytes 3145736 | tf_op jit(solution)/shard_map/ppermute | solution.py:453
  56.0 3.6 %copy-start.2 = (bf16[8,256,128]{2,1,0:T(8,128)(2,1)}, bf16[8,256,128]{2,1,0:T(8,128)(2,1)S(1)}, u32[]{:S(2)}) copy-start(bf16[8,256,128]{2,1,0:T(8,128)(2,1)S(1)} %collective-permute-done.7.refs_16_) | copy-start | bytes 1572868
  56.0 3.6 %copy-start.3 = (bf16[8,256,128]{2,1,0:T(8,128)(2,1)}, bf16[8,256,128]{2,1,0:T(8,128)(2,1)S(1)}, u32[]{:S(2)}) copy-start(bf16[8,256,128]{2,1,0:T(8,128)(2,1)S(1)} %collective-permute-done.6.refs_15_) | copy-start | bytes 1572868
  56.0 3.6 %copy-start.4 = (bf16[8,256,128]{2,1,0:T(8,128)(2,1)}, bf16[8,256,128]{2,1,0:T(8,128)(2,1)S(1)}, u32[]{:S(2)}) copy-start(bf16[8,256,128]{2,1,0:T(8,128)(2,1)S(1)} %collective-permute-done.8.refs_17_) | copy-start | bytes 1572868
  60.8 12.2 %collective-permute-start.13 = (bf16[8,256,128]{2,1,0:T(8,128)(2,1)}, bf16[8,256,128]{2,1,0:T(8,128)(2,1)S(1)}, u32[]{:S(2)}, u32[]{:S(2)}) collective-permute-start(bf16[8,256,128]{2,1,0:T(8,128)(2,1)} %get-tuple-element.87.refs_4_), channel_id=1, source_target_pairs={{16,0},{24,8},{0,16},{8,24},{48,32},{56,40},{32,48},{40,56},{80,64... | collective-permute-start | bytes 1572872 | tf_op jit(solution)/shard_map/ppermute | solution.py:446
  64.1 10.9 %collective-permute-start.12 = (bf16[8,256,128]{2,1,0:T(8,128)(2,1)}, bf16[8,256,128]{2,1,0:T(8,128)(2,1)S(1)}, u32[]{:S(2)}, u32[]{:S(2)}) collective-permute-start(bf16[8,256,128]{2,1,0:T(8,128)(2,1)} %get-tuple-element.86.refs_3_), channel_id=1, source_target_pairs={{96,0},{104,8},{112,16},{120,24},{0,32},{8,40},{16,48},{24,56},{32... | collective-permute-start | bytes 1572872 | tf_op jit(solution)/shard_map/ppermute | solution.py:446
  64.2 10.9 %collective-permute-start.11 = (bf16[8,256,128]{2,1,0:T(8,128)(2,1)}, bf16[8,256,128]{2,1,0:T(8,128)(2,1)S(1)}, u32[]{:S(2)}, u32[]{:S(2)}) collective-permute-start(bf16[8,256,128]{2,1,0:T(8,128)(2,1)} %get-tuple-element.86.refs_3_), channel_id=1, source_target_pairs={{32,0},{40,8},{48,16},{56,24},{64,32},{72,40},{80,48},{88,56},{96,... | collective-permute-start | bytes 1572872 | tf_op jit(solution)/shard_map/ppermute | solution.py:446
  66.8 25.5 %collective-permute-start.10 = (bf16[8,256,256]{2,1,0:T(8,128)(2,1)}, bf16[8,256,256]{2,1,0:T(8,128)(2,1)S(1)}, u32[]{:S(2)}, u32[]{:S(2)}) collective-permute-start(bf16[8,256,256]{2,1,0:T(8,128)(2,1)} %get-tuple-element.64.refs_3_), channel_id=1, source_target_pairs={{3,0},{0,1},{1,2},{2,3},{7,4},{4,5},{5,6},{6,7},{11,8},{8,9},{9,10... | collective-permute-start | bytes 3145736 | tf_op jit(solution)/shard_map/ppermute | solution.py:453
  66.8 25.5 %collective-permute-start.9 = (bf16[8,256,256]{2,1,0:T(8,128)(2,1)}, bf16[8,256,256]{2,1,0:T(8,128)(2,1)}, u32[]{:S(2)}, u32[]{:S(2)}) collective-permute-start(bf16[8,256,256]{2,1,0:T(8,128)(2,1)} %get-tuple-element.65.refs_0_.refs_4_), channel_id=1, source_target_pairs={{1,0},{2,1},{3,2},{0,3},{5,4},{6,5},{7,6},{4,7},{9,8},{10,9},{11,1... | collective-permute-start | bytes 3145736 | tf_op jit(solution)/shard_map/ppermute | solution.py:453
  73.0 2.1 %copy-start.5 = (bf16[8,256,128]{2,1,0:T(8,128)(2,1)}, bf16[8,256,128]{2,1,0:T(8,128)(2,1)S(1)}, u32[]{:S(2)}) copy-start(bf16[8,256,128]{2,1,0:T(8,128)(2,1)S(1)} %collective-permute-done.13.refs_7_) | copy-start | bytes 1572868
  75.1 0.8 copy-start.6
  75.1 1.0 copy-start.7
  80.9 12.5 %collective-permute-start.14 = (bf16[8,8,256,128]{3,2,1,0:T(8,128)(2,1)}, bf16[8,8,256,128]{3,2,1,0:T(8,128)(2,1)}, u32[]{:S(2)}, u32[]{:S(2)}) collective-permute-start(bf16[8,8,256,128]{3,2,1,0:T(8,128)(2,1)} %pack_blocks.1.refs_14_), channel_id=1, source_target_pairs={{8,0},{0,8},{24,16},{16,24},{40,32},{32,40},{56,48},{48,56},{72,64... | collective-permute-start | bytes 12582920 | tf_op jit(solution)/shard_map/ppermute | solution.py:446
  92.3 1.0 copy-start.9
